TPU v7x, 32 devices: a whole 2x2x4 slice. The times are simulated.
32 devices in a mesh: row: 2 (over x), col: 4 (over z), head: 4 (over y, core).
Axes of the slice: x: 2, y: 2, z: 4, core: 2. Of those that a mesh axis runs over, the one named last changes fastest.
Arguments:
- queries: bfloat16 [4, 32, 80, 1024], P('head', None, 'row', 'col'), may hold values from -6.5 to 6.5
- key_vectors: bfloat16 [4, 32, 80, 1024], P('head', None, 'row', 'col'), may hold values from -6.5 to 6.5
- value_vectors: bfloat16 [4, 32, 80, 1024], P('head', None, 'row', 'col'), may hold values from -6 to 6
- gate_logits: bfloat16 [4, 32, 80, 1024], P('head', None, 'row', 'col'), may hold values from -6 to 6
- cotangent: bfloat16 [4, 32, 80, 1024], P('head', None, 'row', 'col'), may hold values from -24 to 24
- pair_normed: bfloat16 [128, 1024, 1024], P('head', 'row', 'col'), may hold values from -6 to 6
- bias_weight: bfloat16 [128, 4], P('head'), may hold values from -0.75 to 0.75
- chain_lengths: int32 [8], replicated, may hold values from 51 to 128, as said below
Outputs:
- query_grad: bfloat16 [4, 32, 80, 1024], P('head', None, 'row', 'col')
- key_grad: bfloat16 [4, 32, 80, 1024], P('head', None, 'row', 'col')
- value_grad: bfloat16 [4, 32, 80, 1024], P('head', None, 'row', 'col')
- gate_grad: bfloat16 [4, 32, 80, 1024], P('head', None, 'row', 'col')
- pair_grad: bfloat16 [128, 1024, 1024], P('head', 'row', 'col')
Inputs may be any that keep to these rules, and one draw needn't show every extreme that they name: `chain_lengths`: every chain has at least one token; positions from the sum of the lengths on are padding.
All inputs are finite; a program needn't handle non-finite values.
Results may differ from a plain program's by a relative error of at most 0.027.
Values may be sent and summed in bfloat16 or wider, within the bound.
A program may use at most 128 MiB of HBM per device.

v0:
```python
import jax
import jax.numpy as jnp
from jax import lax
from jax.sharding import PartitionSpec as P

HEADS = 4
HEAD_DIM = 32
TOKENS = 1024
BLOCK_ROWS = 4


def body(
    queries,
    key_vectors,
    value_vectors,
    gate_logits,
    cotangent,
    pair_normed,
    bias_weight,
    chain_lengths,
):
    score_scale = HEAD_DIM ** (-0.5)
    heads_here = queries.shape[0]
    rows_here = queries.shape[2]
    col_width = queries.shape[3]
    channels_here = pair_normed.shape[0]
    row_block = pair_normed.shape[1]
    col_block = pair_normed.shape[2]
    row_count = lax.axis_size("row")
    col_count = lax.axis_size("col")
    col_index = lax.axis_index("col")
    flat_pair = pair_normed.reshape(channels_here, row_block * col_block)
    partial_value = jnp.dot(bias_weight.T, flat_pair, preferred_element_type=jnp.float32).reshape(
        HEADS, row_block, col_block
    )
    own_bias = lax.psum_scatter(partial_value, "head", scatter_dimension=0, tiled=True)
    pieces = lax.all_gather(own_bias[None], ("row", "col"), axis=0, tiled=True)
    square = pieces.reshape(row_count, col_count, heads_here, row_block, col_block)
    square = square.transpose(2, 0, 3, 1, 4).reshape(heads_here, TOKENS, TOKENS)
    bias_tile = lax.dynamic_slice_in_dim(square, col_index * col_width, col_width, 1)
    keys_all, values_all = (
        lax.all_gather(key_vectors, "col", axis=3, tiled=True),
        lax.all_gather(value_vectors, "col", axis=3, tiled=True),
    )
    token_count = jnp.sum(chain_lengths)
    live_keys = jnp.arange(TOKENS, dtype=jnp.int32) < token_count

    def take_rows(source, first_row):
        return lax.dynamic_slice_in_dim(source, first_row, BLOCK_ROWS, 2)

    def backward_block(bias_grad, block_index):
        first_row = block_index * BLOCK_ROWS
        query_block = take_rows(queries, first_row)
        key_block = take_rows(keys_all, first_row)
        value_block = take_rows(values_all, first_row)
        gate_block = take_rows(gate_logits, first_row).astype(jnp.float32)
        grad_block = take_rows(cotangent, first_row).astype(jnp.float32)
        scores = (
            jnp.einsum(
                "hdij,hdik->hijk", query_block, key_block, preferred_element_type=jnp.float32
            )
            * score_scale
        )
        scores = scores + bias_tile[:, None]
        scores = jnp.where(live_keys[None, None, None, :], scores, -1000000000.0)
        row_max = jnp.max(scores, axis=-1, keepdims=True)
        weights = jnp.exp(scores - row_max)
        attention = weights / jnp.sum(weights, axis=-1, keepdims=True)
        attention_b = attention.astype(jnp.bfloat16)
        attended = jnp.einsum(
            "hijk,hdik->hdij", attention_b, value_block, preferred_element_type=jnp.float32
        )
        gate = jax.nn.sigmoid(gate_block)
        gate_grad = (grad_block * attended * gate * (1.0 - gate)).astype(jnp.bfloat16)
        attended_grad = (grad_block * gate).astype(jnp.bfloat16)
        prob_grad = jnp.einsum(
            "hdij,hdik->hijk", attended_grad, value_block, preferred_element_type=jnp.float32
        )
        row_delta = jnp.sum(attended_grad.astype(jnp.float32) * attended, axis=1)
        score_grad = attention * (prob_grad - row_delta[..., None])
        score_grad_b = score_grad.astype(jnp.bfloat16)
        query_grad = (
            jnp.einsum(
                "hijk,hdik->hdij", score_grad_b, key_block, preferred_element_type=jnp.float32
            )
            * score_scale
        ).astype(jnp.bfloat16)
        key_terms = (
            jnp.einsum(
                "hijk,hdij->hdik", score_grad_b, query_block, preferred_element_type=jnp.float32
            )
            * score_scale
        )
        value_terms = jnp.einsum(
            "hijk,hdij->hdik", attention_b, attended_grad, preferred_element_type=jnp.float32
        )
        return (
            bias_grad + jnp.sum(score_grad, axis=1),
            (query_grad, gate_grad, key_terms, value_terms),
        )

    block_count = rows_here // BLOCK_ROWS
    start_grad = jnp.zeros((heads_here, col_width, TOKENS), jnp.float32)
    bias_rows, stacked = lax.scan(
        backward_block, start_grad, jnp.arange(block_count, dtype=jnp.int32)
    )

    def unstack(source):
        moved = jnp.moveaxis(source, 0, 2)
        return moved.reshape(moved.shape[0], moved.shape[1], rows_here, moved.shape[4])

    query_grad, gate_grad, key_terms, value_terms = [unstack(item) for item in stacked]
    key_sums, value_sums = (
        lax.psum_scatter(key_terms, "col", scatter_dimension=3, tiled=True),
        lax.psum_scatter(value_terms, "col", scatter_dimension=3, tiled=True),
    )
    key_grad = key_sums.astype(jnp.bfloat16)
    value_grad = value_sums.astype(jnp.bfloat16)
    padded_grad = jnp.zeros((heads_here, TOKENS, TOKENS), jnp.float32)
    padded_grad = lax.dynamic_update_slice_in_dim(padded_grad, bias_rows, col_index * col_width, 1)
    blocks = padded_grad.reshape(heads_here, row_count, row_block, col_count, col_block)
    blocks = blocks.transpose(1, 3, 0, 2, 4).reshape(
        row_count * col_count, heads_here, row_block, col_block
    )
    own_grad = lax.psum_scatter(blocks, ("row", "col"), scatter_dimension=0, tiled=True)[0]
    every_head = lax.all_gather(own_grad, "head", axis=0, tiled=True)
    pair_grad = jnp.dot(
        bias_weight.astype(jnp.float32),
        every_head.reshape(HEADS, row_block * col_block),
        precision=lax.Precision.HIGHEST,
    )
    pair_grad = pair_grad.reshape(channels_here, row_block, col_block).astype(jnp.bfloat16)
    return (query_grad, key_grad, value_grad, gate_grad, pair_grad)


def solution(mesh):
    in_specs = (
        P("head", None, "row", "col"),
        P("head", None, "row", "col"),
        P("head", None, "row", "col"),
        P("head", None, "row", "col"),
        P("head", None, "row", "col"),
        P("head", "row", "col"),
        P("head", None),
        P(),
    )
    out_specs = (
        P("head", None, "row", "col"),
        P("head", None, "row", "col"),
        P("head", None, "row", "col"),
        P("head", None, "row", "col"),
        P("head", "row", "col"),
    )
    return jax.shard_map(body, mesh=mesh, in_specs=in_specs, out_specs=out_specs, check_vma=False)
```

profile of v0, /device:TPU:0, one launch (start us, length us, event | category | flops | bytes accessed | tf_op | source)
XLA Modules:
  0.0 823.1 jit_solution(10183980811191681235)
XLA Ops:
  7.9 8.1 fusion.55
  17.7 34.2 %reduce-scatter.5.cloned.1.call-done = f32[1,512,256]{2,1,0:T(8,128)} async-done(((f32[4,512,256]{2,1,0:T(8,128)}), f32[1,512,256]{2,1,0:T(8,128)}) %reduce-scatter.5.cloned.1.call-update) | async-done | bytes 524304 | tf_op jit(solution)/shard_map/reduce_scatter | solution.py:36
  55.1 72.6 %all-gather.11.cloned.1.call-done = f32[8,512,256]{2,1,0:T(8,128)} async-done(((f32[1,512,256]{2,1,0:T(8,128)}), f32[8,512,256]{2,1,0:T(8,128)}) %all-gather.11.cloned.1.call-update) | async-done | bytes 4194320 | tf_op jit(solution)/shard_map/all_gather | solution.py:37
  127.7 6.9 copy.49
  134.7 6.0 reshape.115
  143.0 40.2 %all-gather.7.cloned.1.call-done = bf16[1,32,40,1024]{3,1,2,0:T(8,128)(2,1)} async-done(((bf16[1,32,40,256]{3,1,2,0:T(8,128)(2,1)}), bf16[1,32,40,1024]{3,1,2,0:T(8,128)(2,1)}) %all-gather.7.cloned.1.call-update) | async-done | bytes 2621456 | tf_op jit(solution)/shard_map/all_gather | solution.py:42
  183.1 55.1 %all-gather.9.cloned.1.call-done = bf16[1,32,40,1024]{3,1,2,0:T(8,128)(2,1)} async-done(((bf16[1,32,40,256]{3,1,2,0:T(8,128)(2,1)}), bf16[1,32,40,1024]{3,1,2,0:T(8,128)(2,1)}) %all-gather.9.cloned.1.call-update) | async-done | bytes 2621456 | tf_op jit(solution)/shard_map/all_gather | solution.py:43
  238.3 239.1 %while.19 = (s32[]{:T(128)}, f32[1,256,1024]{2,1,0:T(8,128)S(1)}, bf16[10,1,32,4,256]{4,2,3,1,0:T(8,128)(2,1)}, bf16[10,1,32,4,256]{4,2,3,1,0:T(8,128)(2,1)}, f3...) while((s32[]{:T(128)}, f32[1,256,1024]{2,1,0:T(8,128)S(1)}, ...), condition=%wide.region_7.8_spmd.clone, body=%wide.region_2.7_spmd.clone.sunk | while | flops 416809984 | bytes 50749724 | solution.py:104
  265.0 4.9 fusion.92
  288.9 4.9 fusion.92
  312.8 4.9 fusion.92
  336.7 4.9 fusion.92
  360.6 4.9 fusion.92
  408.5 5.0 fusion.92
  481.0 5.7 reshape.120
  486.7 5.0 copy.58
  492.0 7.9 copy.61
  499.9 7.9 copy.62
  508.2 69.9 %reduce-scatter.11.cloned.1.call-done = f32[1,1,512,256]{3,2,0,1:T(8,128)} async-done(((f32[8,1,512,256]{3,2,0,1:T(8,128)}), f32[1,1,512,256]{3,2,0,1:T(8,128)}) %reduce-scatter.11.cloned.1.call-update) | async-done | bytes 524304 | tf_op jit(solution)/shard_map/reduce_scatter | solution.py:125
  581.6 92.2 %reduce-scatter.7.cloned.1.call-done = f32[1,32,40,256]{3,2,1,0:T(8,128)} async-done(((f32[1,32,40,1024]{3,2,1,0:T(8,128)}), f32[1,32,40,256]{3,2,1,0:T(8,128)}) %reduce-scatter.7.cloned.1.call-update) | async-done | bytes 1310736 | tf_op jit(solution)/shard_map/reduce_scatter | solution.py:114
  676.0 95.0 %reduce-scatter.9.cloned.1.call-done = f32[1,32,40,256]{3,2,1,0:T(8,128)} async-done(((f32[1,32,40,1024]{3,2,1,0:T(8,128)}), f32[1,32,40,256]{3,2,1,0:T(8,128)}) %reduce-scatter.9.cloned.1.call-update) | async-done | bytes 1310736 | tf_op jit(solution)/shard_map/reduce_scatter | solution.py:115
  773.1 22.5 %all-gather.13.cloned.1.call-done = f32[4,1,512,256]{3,2,1,0:T(8,128)} async-done(((f32[1,1,512,256]{3,2,1,0:T(8,128)}), f32[4,1,512,256]{3,2,1,0:T(8,128)}) %all-gather.13.cloned.1.call-update) | async-done | bytes 2097168 | tf_op jit(solution)/shard_map/all_gather | solution.py:126
  798.5 9.0 %convolution_convert_fusion = bf16[131072,32]{0,1:T(8,128)(2,1)} fusion(f32[4,131072]{1,0:T(4,128)S(1)} %bitcast.163, bf16[32,4]{0,1:T(4,128)(2,1)S(1)} %copy-done), kind=kOutput, calls=%fused_computation.61 | convolution fusion | flops 205520896 | bytes 10486016 | tf_op jit(solution)/shard_map/dot_general | solution.py:127
  807.5 8.8 %copy.70 = bf16[4,8,512,256]{3,2,1,0:T(8,128)(2,1)} copy(bf16[4,8,512,256]{3,1,2,0:T(8,128)(2,1)} %bitcast.160) | data formatting | bytes 16777216
  (188 shorter events, 225.3 us)
Async XLA Ops:
  7.2 0.7 copy-start
  7.2 44.8 %reduce-scatter.5.cloned.1.call-start = ((), (), s32[]{:S(2)}) async-start(), calls=%async_computation.5 | async-start | bytes 2621440 | tf_op jit(solution)/shard_map/reduce_scatter | solution.py:36
  16.0 36.1 %copy-start.2 = (bf16[1,32,40,256]{3,2,1,0:T(8,128)(2,1)S(1)}, bf16[1,32,40,256]{3,2,1,0:T(8,128)(2,1)}, u32[]{:S(2)}) copy-start(bf16[1,32,40,256]{3,2,1,0:T(8,128)(2,1)} %param.11) | copy-start | bytes 1966084
  16.0 37.2 %copy-start.3 = (bf16[1,32,40,256]{3,2,1,0:T(8,128)(2,1)S(1)}, bf16[1,32,40,256]{3,2,1,0:T(8,128)(2,1)}, u32[]{:S(2)}) copy-start(bf16[1,32,40,256]{3,2,1,0:T(8,128)(2,1)} %param.12) | copy-start | bytes 1966084
  17.7 36.8 %copy-start.5 = (s32[8]{0:T(128)S(1)}, s32[8]{0:T(128)}, u32[]{:S(2)}) copy-start(s32[8]{0:T(128)} %param.17) | copy-start | bytes 100
  17.7 110.0 %all-gather.11.cloned.1.call-start = ((), (), s32[]{:S(2)}) async-start(), calls=%async_computation.10 | async-start | bytes 4718592 | tf_op jit(solution)/shard_map/all_gather | solution.py:37
  52.0 131.1 %all-gather.7.cloned.1.call-start = ((), (), s32[]{:S(2)}) async-start(), calls=%async_computation.4 | async-start | bytes 3276800 | tf_op jit(solution)/shard_map/all_gather | solution.py:42
  53.1 185.2 %all-gather.9.cloned.1.call-start = ((), (), s32[]{:S(2)}) async-start(), calls=%async_computation.6 | async-start | bytes 3276800 | tf_op jit(solution)/shard_map/all_gather | solution.py:43
  54.1 523.9 %reduce-scatter.11.cloned.1.call-start = ((), (), s32[]{:S(2)}) async-start(), calls=%async_computation.9 | async-start | bytes 4718592 | tf_op jit(solution)/shard_map/reduce_scatter | solution.py:125
  246.0 5.6 copy-start.1
  269.9 5.6 copy-start.1
  293.9 5.6 copy-start.1
  317.8 5.6 copy-start.1
  341.7 5.6 copy-start.1
  365.6 5.6 copy-start.1
  389.5 5.6 copy-start.1
  413.4 5.6 copy-start.1
  437.3 5.6 copy-start.1
  461.2 5.6 copy-start.1
  491.7 182.0 %reduce-scatter.7.cloned.1.call-start = ((), (), s32[]{:S(2)}) async-start(), calls=%async_computation.7 | async-start | bytes 6553600 | tf_op jit(solution)/shard_map/reduce_scatter | solution.py:114
  499.9 271.0 %reduce-scatter.9.cloned.1.call-start = ((), (), s32[]{:S(2)}) async-start(), calls=%async_computation.8 | async-start | bytes 6553600 | tf_op jit(solution)/shard_map/reduce_scatter | solution.py:115
  507.8 70.2 %copy-start.4 = (bf16[10,1,32,4,256]{4,2,3,1,0:T(8,128)(2,1)S(1)}, bf16[10,1,32,4,256]{4,2,3,1,0:T(8,128)(2,1)}, u32[]{:S(2)}) copy-start(bf16[10,1,32,4,256]{4,2,3,1,0:T(8,128)(2,1)} %get-tuple-element.81) | copy-start | bytes 1966084
  507.9 287.7 %all-gather.13.cloned.1.call-start = ((), (), s32[]{:S(2)}) async-start(), calls=%async_computation.11 | async-start | bytes 2621440 | tf_op jit(solution)/shard_map/all_gather | solution.py:126
Sparse Core Ops, SparseCore 0:
  17.8 34.1 reduce-scatter.4
  54.3 73.3 all-gather.10
  130.0 53.1 all-gather.6
  185.2 53.0 all-gather.8
  491.9 86.1 reduce-scatter.10
  580.2 93.5 reduce-scatter.6
  676.6 94.2 reduce-scatter.8
  772.5 23.0 all-gather.12
where the time goes:
time: 826 us; the launch traced here: 823 us
  waiting for transfers between devices  482 us (58%)
  matrix products  166 us (20%)
  local copies, waits for them, and re-layouts  90.7 us (11%)
  other arithmetic  62.6 us (8%)
  between operations  14.2 us (2%)
    reduce_scatter x1, waiting for transfers between devices, body(): lax.psum_scatter(value_terms, 'col', scatter_dimension=3, tiled=True)  95 us
    reduce_scatter x1, waiting for transfers between devices, body(): lax.psum_scatter(key_terms, 'col', scatter_dimension=3, tiled=True)  92.2 us
    all_gather x1, waiting for transfers between devices, body(): pieces = lax.all_gather(own_bias[None], ('row', 'col'), axis=0, tiled=True)  72.6 us
    reduce_scatter x1, waiting for transfers between devices, body(): lax.psum_scatter(blocks, ('row', 'col'), scatter_dimension=0, tiled=True)[0]  69.9 us
    all_gather x1, waiting for transfers between devices, body(): lax.all_gather(value_vectors, 'col', axis=3, tiled=True)  55.1 us
    sub x10, matrix products, backward_block(): weights = jnp.exp(scores - row_max)  49.5 us
    all_gather x1, waiting for transfers between devices, body(): lax.all_gather(key_vectors, 'col', axis=3, tiled=True)  40.2 us
    reduce_scatter x1, waiting for transfers between devices, body(): lax.psum_scatter(partial_value, 'head', scatter_dimension=0, tiled=True)  34.2 us
  transfers between devices with their start and end apart: 8, of which 8 were waited for; matrix products, arithmetic and copies ran while one was open for 5% of the time, Pallas kernels for 0%

commit v1 on v0

v1 whole, which is shorter than its diff:
```python
import functools

import jax
import jax.numpy as jnp
from jax import lax
from jax.experimental import pallas as pl
from jax.experimental.pallas import tpu as pltpu
from jax.sharding import PartitionSpec as P

HEADS = 4
HEAD_DIM = 32
TOKENS = 1024
SCALE = HEAD_DIM ** (-0.5)
LOG2E = 1.4426950408889634
KEY_BLOCK = 256
CHUNK_ROWS = 10
NEG = -1000000000.0


def contract(left, right, left_dim, right_dim):
    return lax.dot_general(
        left, right, (((left_dim,), (right_dim,)), ((), ())), preferred_element_type=jnp.float32
    )


def attention_kernel(
    count_ref, q_ref, kv_ref, gate_ref, cot_ref, bias_ref, start_ref,
    dq_ref, dgate_ref, dkv_ref, grad_ref, s_ref,
):
    cols, _, _, width = kv_ref.shape
    tokens = cols * width
    blocks = tokens // KEY_BLOCK
    per_block = KEY_BLOCK // width
    d = HEAD_DIM

    @pl.when(pl.program_id(0) == 0)
    def _():
        grad_ref[...] = start_ref[...]

    def load(block, low):
        parts = [kv_ref[block * per_block + n, 0, low:low + d, :] for n in range(per_block)]
        return parts[0] if per_block == 1 else jnp.concatenate(parts, axis=1)

    def store(block, low, value):
        for n in range(per_block):
            piece = value[:, n * width:(n + 1) * width]
            dkv_ref[block * per_block + n, 0, low:low + d, :] = piece.astype(jnp.bfloat16)

    def variant(live_blocks):
        q = q_ref[0]
        top = None
        for b in range(live_blocks):
            rows = pl.ds(b * KEY_BLOCK, KEY_BLOCK)
            s = contract(load(b, 0), q, 0, 0) * (SCALE * LOG2E) + bias_ref[rows, :]
            s_ref[rows, :] = s
            block_top = jnp.max(s, axis=0, keepdims=True)
            top = block_top if top is None else jnp.maximum(top, block_top)
        total = jnp.zeros_like(top)
        for b in range(live_blocks):
            rows = pl.ds(b * KEY_BLOCK, KEY_BLOCK)
            p = jnp.exp2(s_ref[rows, :] - top)
            s_ref[rows, :] = p
            total = total + jnp.sum(p, axis=0, keepdims=True)
        inverse = 1.0 / total
        gate = 1.0 / (1.0 + jnp.exp(-gate_ref[0].astype(jnp.float32)))
        cot = cot_ref[0].astype(jnp.float32)
        out_grad = (cot * gate).astype(jnp.bfloat16)
        attended = jnp.zeros(q.shape, jnp.float32)
        for b in range(live_blocks):
            rows = pl.ds(b * KEY_BLOCK, KEY_BLOCK)
            p = s_ref[rows, :] * inverse
            s_ref[rows, :] = p
            pb = p.astype(jnp.bfloat16)
            attended = attended + contract(load(b, d), pb, 1, 0)
            store(b, d, contract(out_grad, pb, 1, 1))
        dgate_ref[0] = (cot * attended * gate * (1.0 - gate)).astype(jnp.bfloat16)
        delta = jnp.sum(out_grad.astype(jnp.float32) * attended, axis=0, keepdims=True)
        dq = jnp.zeros(q.shape, jnp.float32)
        for b in range(live_blocks):
            rows = pl.ds(b * KEY_BLOCK, KEY_BLOCK)
            dp = contract(load(b, d), out_grad, 0, 0)
            ds = s_ref[rows, :] * (dp - delta)
            grad_ref[rows, :] = grad_ref[rows, :] + ds
            dsb = ds.astype(jnp.bfloat16)
            dq = dq + contract(load(b, 0), dsb, 1, 0)
            store(b, 0, contract(q, dsb, 1, 1) * SCALE)
        dq_ref[0] = (dq * SCALE).astype(jnp.bfloat16)
        for b in range(live_blocks, blocks):
            dead = jnp.zeros((d, KEY_BLOCK), jnp.float32)
            store(b, 0, dead)
            store(b, d, dead)

    count = count_ref[0]
    for live in range(1, blocks + 1):
        low = (live - 1) * KEY_BLOCK
        high = live * KEY_BLOCK

        @pl.when((count > low) & (count <= high))
        def _(live=live):
            variant(live)


def attention_chunk(count, q, kv, gate, cot, bias, start):
    rows, d, width = q.shape
    cols = kv.shape[0]
    kv_width = kv.shape[3]
    tokens = cols * kv_width
    row_spec = pl.BlockSpec((1, d, width), lambda i: (i, 0, 0))
    kv_spec = pl.BlockSpec((cols, 1, 2 * d, kv_width), lambda i: (0, i, 0, 0))
    square_spec = pl.BlockSpec((tokens, width), lambda i: (0, 0))
    small = jax.ShapeDtypeStruct(q.shape, jnp.bfloat16)
    return pl.pallas_call(
        attention_kernel,
        grid=(rows,),
        in_specs=[
            pl.BlockSpec(memory_space=pltpu.SMEM),
            row_spec, kv_spec, row_spec, row_spec, square_spec, square_spec,
        ],
        out_specs=[row_spec, row_spec, kv_spec, square_spec],
        out_shape=[
            small, small,
            jax.ShapeDtypeStruct(kv.shape, jnp.bfloat16),
            jax.ShapeDtypeStruct((tokens, width), jnp.float32),
        ],
        scratch_shapes=[pltpu.VMEM((tokens, width), jnp.float32)],
        compiler_params=pltpu.CompilerParams(vmem_limit_bytes=40 * 1024 * 1024),
        cost_estimate=pl.CostEstimate(
            flops=12 * rows * d * tokens * width,
            bytes_accessed=4 * rows * d * (2 * tokens + 2 * width) + 12 * tokens * width,
            transcendentals=rows * tokens * width,
        ),
    )(count, q, kv, gate, cot, bias, start)


def body(
    queries,
    key_vectors,
    value_vectors,
    gate_logits,
    cotangent,
    pair_normed,
    bias_weight,
    chain_lengths,
):
    rows_here = queries.shape[2]
    width = queries.shape[3]
    channels_here, row_block, col_block = pair_normed.shape
    col_count = lax.axis_size("col")
    count = jnp.sum(chain_lengths).reshape(1)

    def rows_first(source):
        return source[0].transpose(1, 0, 2)

    kv = jnp.concatenate([rows_first(key_vectors), rows_first(value_vectors)], axis=1)
    starts = list(range(0, rows_here, CHUNK_ROWS))
    gathered = [
        lax.all_gather(kv[a:a + CHUNK_ROWS], "col", axis=0, tiled=False) for a in starts
    ]

    flat_pair = pair_normed.reshape(channels_here, row_block * col_block)
    partial = jnp.dot(bias_weight.T, flat_pair, preferred_element_type=jnp.float32)
    partial = partial.astype(jnp.float16).reshape(HEADS, row_block, col_block)
    parts = lax.all_to_all(partial, "head", split_axis=0, concat_axis=0, tiled=True)
    own_bias = jnp.sum(parts.astype(jnp.float32), axis=0).astype(jnp.float16)
    tall = lax.all_gather(own_bias, "row", axis=0, tiled=True)
    wide = lax.all_to_all(tall, "col", split_axis=0, concat_axis=1, tiled=True)
    live = jnp.arange(TOKENS, dtype=jnp.int32)[:, None] < count[0]
    bias = jnp.where(live, wide.T.astype(jnp.float32) * LOG2E, NEG)

    q, gate, cot = rows_first(queries), rows_first(gate_logits), rows_first(cotangent)
    total = jnp.zeros((TOKENS, width), jnp.float32)
    dq, dgate, dkv = [], [], []
    for a, keys in zip(starts, gathered):
        part = slice(a, a + CHUNK_ROWS)
        dq_part, dgate_part, dkv_part, total = attention_chunk(
            count, q[part], keys, gate[part], cot[part], bias, total
        )
        dq.append(dq_part)
        dgate.append(dgate_part)
        dkv.append(lax.psum_scatter(dkv_part, "col", scatter_dimension=0, tiled=False))

    def rows_last(parts):
        return jnp.concatenate(parts, axis=0).transpose(1, 0, 2)[None]

    query_grad, gate_grad = rows_last(dq), rows_last(dgate)
    both = jnp.concatenate(dkv, axis=0).transpose(1, 0, 2)
    key_grad, value_grad = both[None, :HEAD_DIM], both[None, HEAD_DIM:]

    square = total.astype(jnp.bfloat16).T
    tall_grad = lax.all_to_all(square, "col", split_axis=1, concat_axis=0, tiled=True)
    own_grad = lax.psum_scatter(tall_grad, "row", scatter_dimension=0, tiled=True)
    every_head = lax.all_gather(own_grad, "head", axis=0, tiled=False)
    pair_grad = jnp.dot(
        bias_weight,
        every_head.reshape(HEADS, row_block * col_block),
        preferred_element_type=jnp.float32,
    )
    pair_grad = pair_grad.reshape(channels_here, row_block, col_block).astype(jnp.bfloat16)
    return (query_grad, key_grad, value_grad, gate_grad, pair_grad)


def solution(mesh):
    in_specs = (
        P("head", None, "row", "col"),
        P("head", None, "row", "col"),
        P("head", None, "row", "col"),
        P("head", None, "row", "col"),
        P("head", None, "row", "col"),
        P("head", "row", "col"),
        P("head", None),
        P(),
    )
    out_specs = (
        P("head", None, "row", "col"),
        P("head", None, "row", "col"),
        P("head", None, "row", "col"),
        P("head", None, "row", "col"),
        P("head", "row", "col"),
    )
    return jax.shard_map(body, mesh=mesh, in_specs=in_specs, out_specs=out_specs, check_vma=False)
```

time: 826 us -> 380 us (0.46)
  waiting for transfers between devices: 482 us -> 196 us
  matrix products: 166 us -> 10.2 us
  Pallas kernels: 0 us -> 70.4 us
  other arithmetic: 62.6 us -> 6.84 us
  local copies, waits for them, and re-layouts: 90.7 us -> 46.2 us
  blocking collectives: 0 us -> 26.4 us
  starting transfers between devices: 0.99 us -> 10.1 us
    all_gather x4 -> x5, waiting for transfers between devices: 190 us -> 15 us  [the longest x1 13.1 us: body(): every_head = lax.all_gather(own_grad, 'head', axis=0, tiled=False)]
    reduce_scatter x4 -> x5, waiting for transfers between devices: 291 us -> 140 us  [the longest x4 129 us: body(): lax.psum_scatter(dkv_part, 'col', scatter_dimension=0, tiled=False)]
    dot_general x51 -> x1, matrix products: 108 us -> 5.64 us  [body(): jnp.dot(bias_weight, every_head.reshape(HEADS, row_block * col_block), pr...]
    pallas_call x0 -> x4, Pallas kernels: none -> 70.4 us  [attention_chunk(): pl.pallas_call(attention_kernel, grid=(rows,), in_specs=[pl.BlockSpec(mem...]
    sub x10 -> x0, matrix products: 49.5 us -> none  [backward_block(): weights = jnp.exp(scores - row_max)]
    all_to_all x0 -> x2, waiting for transfers between devices: none -> 37.2 us  [the longest x1 23.3 us: body(): wide = lax.all_to_all(tall, 'col', split_axis=0, concat_axis=1, tiled=True)]
    convert_element_type x12 -> x2, other arithmetic: 33 us -> 0.09 us  [the longest x1 0.05 us: body(): square = total.astype(jnp.bfloat16).T]
    reshape x6 -> x1, local copies, waits for them, and re-layouts: 30.9 us -> 2 us  [body(): every_head.reshape(HEADS, row_block * col_block)]
  transfers between devices with their start and end apart: 8 -> 12, of which waited for: 8 -> 9; matrix products, arithmetic and copies ran while one was open for 5% -> 8% of each run, Pallas kernels for 0% -> 14%
where the time goes in v1:
time: 380 us; the launch traced here: 381 us
  waiting for transfers between devices  196 us (52%)
  Pallas kernels  70.4 us (19%)
  local copies, waits for them, and re-layouts  46.2 us (12%)
  blocking collectives  26.4 us (7%)
  between operations  14.3 us (4%)
  matrix products  10.2 us (3%)
  starting transfers between devices  10.1 us (3%)
  other arithmetic  6.84 us (2%)
    reduce_scatter x4, waiting for transfers between devices, body(): lax.psum_scatter(dkv_part, 'col', scatter_dimension=0, tiled=False)  129 us
    pallas_call x4, Pallas kernels, attention_chunk(): pl.pallas_call(attention_kernel, grid=(rows,), in_specs=[pl.BlockSpec(mem...  70.4 us
    unnamed x42, local copies, waits for them, and re-layouts  40.8 us
    all_to_all x1, waiting for transfers between devices, body(): wide = lax.all_to_all(tall, 'col', split_axis=0, concat_axis=1, tiled=True)  23.3 us
    all_to_all x1, blocking collectives, body(): lax.all_to_all(square, 'col', split_axis=1, concat_axis=0, tiled=True)  17.2 us
    all_to_all x1, waiting for transfers between devices, body(): lax.all_to_all(partial, 'head', split_axis=0, concat_axis=0, tiled=True)  13.9 us
    all_gather x1, waiting for transfers between devices, body(): every_head = lax.all_gather(own_grad, 'head', axis=0, tiled=False)  13.1 us
    reduce_scatter x1, waiting for transfers between devices, body(): lax.psum_scatter(tall_grad, 'row', scatter_dimension=0, tiled=True)  10.9 us
  transfers between devices with their start and end apart: 12, of which 9 were waited for; matrix products, arithmetic and copies ran while one was open for 8% of the time, Pallas kernels for 14%

profile of v1, /device:TPU:0, one launch (start us, length us, event | category | flops | bytes accessed | tf_op | source)
XLA Modules:
  0.0 380.8 jit_solution(16261684145789333468)
XLA Ops:
  7.2 1.6 copy_bitcast_fusion.3
  11.4 11.6 %copy.48 = bf16[4,8,512,256]{3,1,2,0:T(8,128)(2,1)} copy(bf16[4,8,512,256]{3,2,1,0:T(8,128)(2,1)} %bitcast.81) | data formatting | bytes 16777216
  23.0 4.6 %convolution_convert_fusion.1 = f16[4,131072]{1,0:T(4,128)(2,1)S(1)} fusion(bf16[32,4]{0,1:T(4,128)(2,1)S(1)} %copy-done, bf16[32,131072]{1,0:T(8,128)(2,1)} %bitcast.80), kind=kOutput, calls=%fused_computation.1 | convolution fusion | flops 34078720 | bytes 9437440 | tf_op jit(solution)/shard_map/dot_general | solution.py:161
  28.9 4.2 %all-to-all-start = ((f16[4,512,256]{2,1,0:T(8,128)(2,1)}), f16[4,512,256]{2,1,0:T(8,128)(2,1)S(1)}, u32[]{:S(2)}, u32[]{:S(2)}) async-start(f16[4,512,256]{2,1,0:T(8,128)(2,1)} %bitcast.67), calls=%async_computation | async-start | bytes 2097152 | tf_op jit(solution)/shard_map/all_to_all | solution.py:163
  33.7 13.9 %all-to-all-done = f16[4,512,256]{2,1,0:T(8,128)(2,1)S(1)} async-done(((f16[4,512,256]{2,1,0:T(8,128)(2,1)}), f16[4,512,256]{2,1,0:T(8,128)(2,1)S(1)}, u32[]{:S(2)}, u32[]{:S(2)}) %all-to-all-start) | async-done | bytes 1048608 | tf_op jit(solution)/shard_map/all_to_all | solution.py:163
  47.8 9.2 %all_gather.35 = f16[1024,256]{1,0:T(8,128)(2,1)} all-gather(f16[512,256]{1,0:T(8,128)(2,1)S(1)} %convert_element_type.29), channel_id=1, replica_groups=mesh['row'=2,'col'=4,'head'=4] {'row'}, dimensions={0}, use_global_device_ids=true | all-gather | bytes 786432 | tf_op jit(solution)/shard_map/all_gather | solution.py:165
  57.0 5.3 %all-to-all-start.1 = ((f16[4,256,256]{2,1,0:T(8,128)(2,1)}), f16[4,256,256]{2,1,0:T(8,128)(2,1)}, u32[]{:S(2)}, u32[]{:S(2)}) async-start(f16[4,256,256]{2,1,0:T(8,128)(2,1)} %bitcast.12), calls=%async_computation.1 | async-start | bytes 1048576 | tf_op jit(solution)/shard_map/all_to_all | solution.py:166
  66.2 23.3 %all-to-all-done.1 = f16[4,256,256]{2,1,0:T(8,128)(2,1)} async-done(((f16[4,256,256]{2,1,0:T(8,128)(2,1)}), f16[4,256,256]{2,1,0:T(8,128)(2,1)}, u32[]{:S(2)}, u32[]{:S(2)}) %all-to-all-start.1) | async-done | bytes 524320 | tf_op jit(solution)/shard_map/all_to_all | solution.py:166
  94.9 17.7 %shard_map.119 = (bf16[10,32,256]{2,1,0:T(8,128)(2,1)S(1)}, bf16[10,32,256]{2,1,0:T(8,128)(2,1)S(1)}, bf16[4,10,64,256]{3,2,1,0:T(8,128)(2,1)}, f32[1024,256]{1,0:T(8,128)S(1)}) custom-call(s32[1]{0:T(128)} %bitcast.count_ref, bf16[10,32,256]{2,1,0:T(8,128)(2,1)S(1)} %get-tuple-element.66.q_ref, bf16[4,10,64,256]{3,2,1,0:T(8,128)(2,1)S(1)} %bitcast.78, ...), custom_call_target="tpu_custom_call" | custom-call | flops 1006632960 | bytes 6422528 | tf_op jit(solution)/shard_map/pallas_call | solution.py:112
  116.1 17.5 %shard_map.120 = (bf16[10,32,256]{2,1,0:T(8,128)(2,1)S(1)}, bf16[10,32,256]{2,1,0:T(8,128)(2,1)S(1)}, bf16[4,10,64,256]{3,2,1,0:T(8,128)(2,1)}, f32[1024,256]{1,0:T(8,128)S(1)}) custom-call(s32[1]{0:T(128)} %bitcast.count_ref, bf16[10,32,256]{2,1,0:T(8,128)(2,1)S(1)} %get-tuple-element.69.q_ref, bf16[4,10,64,256]{3,2,1,0:T(8,128)(2,1)S(1)} %bitcast.76, ...), custom_call_target="tpu_custom_call" | custom-call | flops 1006632960 | bytes 6422528 | tf_op jit(solution)/shard_map/pallas_call | solution.py:112
  137.2 17.6 %shard_map.121 = (bf16[10,32,256]{2,1,0:T(8,128)(2,1)S(1)}, bf16[10,32,256]{2,1,0:T(8,128)(2,1)S(1)}, bf16[4,10,64,256]{3,2,1,0:T(8,128)(2,1)}, f32[1024,256]{1,0:T(8,128)S(1)}) custom-call(s32[1]{0:T(128)} %bitcast.count_ref, bf16[10,32,256]{2,1,0:T(8,128)(2,1)S(1)} %get-tuple-element.68.q_ref, bf16[4,10,64,256]{3,2,1,0:T(8,128)(2,1)S(1)} %bitcast.75, ...), custom_call_target="tpu_custom_call" | custom-call | flops 1006632960 | bytes 6422528 | tf_op jit(solution)/shard_map/pallas_call | solution.py:112
  155.7 1.9 all-gather.17.cloned.1.call-done
  160.2 17.6 %shard_map.122 = (bf16[10,32,256]{2,1,0:T(8,128)(2,1)S(1)}, bf16[10,32,256]{2,1,0:T(8,128)(2,1)S(1)}, bf16[4,10,64,256]{3,2,1,0:T(8,128)(2,1)}, f32[1024,256]{1,0:T(8,128)S(1)}) custom-call(s32[1]{0:T(128)} %bitcast.count_ref, bf16[10,32,256]{2,1,0:T(8,128)(2,1)S(1)} %get-tuple-element.67.q_ref, bf16[4,10,64,256]{3,2,1,0:T(8,128)(2,1)S(1)} %bitcast.77, ...), custom_call_target="tpu_custom_call" | custom-call | flops 1006632960 | bytes 6422528 | tf_op jit(solution)/shard_map/pallas_call | solution.py:112
  178.0 17.2 %all_to_all.37 = bf16[256,4,256]{2,0,1:T(8,128)(2,1)} all-to-all(bf16[256,4,256]{2,0,1:T(8,128)(2,1)S(1)} %copy.43), channel_id=1, replica_groups=mesh['row'=2,'col'=4,'head'=4] {'col'}, dimensions={1} | all-to-all | bytes 1048576 | tf_op jit(solution)/shard_map/all_to_all | solution.py:190
  198.1 10.9 %reduce-scatter.14.cloned.1.call-done = bf16[512,256]{1,0:T(8,128)(2,1)} async-done(((bf16[1024,256]{1,0:T(8,128)(2,1)}), bf16[512,256]{1,0:T(8,128)(2,1)}) %reduce-scatter.14.cloned.1.call-update) | async-done | bytes 262160 | tf_op jit(solution)/shard_map/reduce_scatter | solution.py:191
  211.6 31.5 %reduce-scatter.6.cloned.1.call-done = bf16[1,10,64,256]{3,2,1,0:T(8,128)(2,1)} async-done(((bf16[4,10,64,256]{3,2,1,0:T(8,128)(2,1)}), bf16[1,10,64,256]{3,2,1,0:T(8,128)(2,1)}) %reduce-scatter.6.cloned.1.call-update) | async-done | bytes 327696 | tf_op jit(solution)/shard_map/reduce_scatter | solution.py:180
  243.1 32.4 %reduce-scatter.8.cloned.1.call-done = bf16[1,10,64,256]{3,2,1,0:T(8,128)(2,1)} async-done(((bf16[4,10,64,256]{3,2,1,0:T(8,128)(2,1)}), bf16[1,10,64,256]{3,2,1,0:T(8,128)(2,1)}) %reduce-scatter.8.cloned.1.call-update) | async-done | bytes 327696 | tf_op jit(solution)/shard_map/reduce_scatter | solution.py:180
  275.6 32.4 %reduce-scatter.12.cloned.1.call-done = bf16[1,10,64,256]{3,2,1,0:T(8,128)(2,1)} async-done(((bf16[4,10,64,256]{3,2,1,0:T(8,128)(2,1)}), bf16[1,10,64,256]{3,2,1,0:T(8,128)(2,1)}) %reduce-scatter.12.cloned.1.call-update) | async-done | bytes 327696 | tf_op jit(solution)/shard_map/reduce_scatter | solution.py:180
  308.0 32.5 %reduce-scatter.10.cloned.1.call-done = bf16[1,10,64,256]{3,2,1,0:T(8,128)(2,1)} async-done(((bf16[4,10,64,256]{3,2,1,0:T(8,128)(2,1)}), bf16[1,10,64,256]{3,2,1,0:T(8,128)(2,1)}) %reduce-scatter.10.cloned.1.call-update) | async-done | bytes 327696 | tf_op jit(solution)/shard_map/reduce_scatter | solution.py:180
  340.5 1.4 maximum_bitcast_fusion
  344.4 13.1 %all-gather.19.cloned.1.call-done = bf16[2048,256]{1,0:T(8,128)(2,1)} async-done(((bf16[512,256]{1,0:T(8,128)(2,1)}), bf16[2048,256]{1,0:T(8,128)(2,1)}) %all-gather.19.cloned.1.call-update) | async-done | bytes 1048592 | tf_op jit(solution)/shard_map/all_gather | solution.py:192
  357.5 2.0 reshape.41
  359.5 5.6 %convolution_convert_fusion = bf16[131072,32]{0,1:T(8,128)(2,1)} fusion(bf16[4,131072]{1,0:T(4,128)(2,1)S(1)} %reshape.41, bf16[32,4]{0,1:T(4,128)(2,1)S(1)} %copy-done), kind=kOutput, calls=%fused_computation | convolution fusion | flops 37748736 | bytes 9437440 | tf_op jit(solution)/shard_map/dot_general | solution.py:193
  365.1 8.8 %copy.50 = bf16[4,8,512,256]{3,2,1,0:T(8,128)(2,1)} copy(bf16[4,8,512,256]{3,1,2,0:T(8,128)(2,1)} %bitcast.79) | data formatting | bytes 16777216
  (79 shorter events, 32.5 us)
Async XLA Ops:
  7.2 15.9 %copy-start = (bf16[32,4]{0,1:T(4,128)(2,1)S(1)}, bf16[32,4]{0,1:T(4,128)(2,1)}, u32[]{:S(2)}) copy-start(bf16[32,4]{0,1:T(4,128)(2,1)} %param.14) | copy-start | bytes 772
  7.2 86.3 %all-gather.11.cloned.1.call-start = ((), (), s32[]{:S(2)}) async-start(), calls=%async_computation.13 | async-start | bytes 1638400 | tf_op jit(solution)/shard_map/all_gather | solution.py:157
  9.9 103.6 %all-gather.13.cloned.1.call-start = ((), (), s32[]{:S(2)}) async-start(), calls=%async_computation.14 | async-start | bytes 1638400 | tf_op jit(solution)/shard_map/all_gather | solution.py:157
  10.7 124.0 %all-gather.15.cloned.1.call-start = ((), (), s32[]{:S(2)}) async-start(), calls=%async_computation.15 | async-start | bytes 1638400 | tf_op jit(solution)/shard_map/all_gather | solution.py:157
  28.9 18.7 %all-to-all-start = ((f16[4,512,256]{2,1,0:T(8,128)(2,1)}), f16[4,512,256]{2,1,0:T(8,128)(2,1)S(1)}, u32[]{:S(2)}, u32[]{:S(2)}) async-start(f16[4,512,256]{2,1,0:T(8,128)(2,1)} %bitcast.67), calls=%async_computation | async-start | bytes 2097152 | tf_op jit(solution)/shard_map/all_to_all | solution.py:163
  33.1 124.5 %all-gather.17.cloned.1.call-start = ((), (), s32[]{:S(2)}) async-start(), calls=%async_computation.16 | async-start | bytes 1638400 | tf_op jit(solution)/shard_map/all_gather | solution.py:157
  47.8 14.6 %copy-start.12 = (bf16[1,32,40,256]{3,2,1,0:T(8,128)(2,1)S(1)}, bf16[1,32,40,256]{3,2,1,0:T(8,128)(2,1)}, u32[]{:S(2)}) copy-start(bf16[1,32,40,256]{3,2,1,0:T(8,128)(2,1)} %param.8) | copy-start | bytes 1966084
  57.0 5.5 %copy-start.13 = (bf16[1,32,40,256]{3,2,1,0:T(8,128)(2,1)S(1)}, bf16[1,32,40,256]{3,2,1,0:T(8,128)(2,1)}, u32[]{:S(2)}) copy-start(bf16[1,32,40,256]{3,2,1,0:T(8,128)(2,1)} %param.11) | copy-start | bytes 1966084
  57.0 32.5 %all-to-all-start.1 = ((f16[4,256,256]{2,1,0:T(8,128)(2,1)}), f16[4,256,256]{2,1,0:T(8,128)(2,1)}, u32[]{:S(2)}, u32[]{:S(2)}) async-start(f16[4,256,256]{2,1,0:T(8,128)(2,1)} %bitcast.12), calls=%async_computation.1 | async-start | bytes 1048576 | tf_op jit(solution)/shard_map/all_to_all | solution.py:166
  62.3 146.7 %reduce-scatter.14.cloned.1.call-start = ((), (), s32[]{:S(2)}) async-start(), calls=%async_computation.12 | async-start | bytes 786432 | tf_op jit(solution)/shard_map/reduce_scatter | solution.py:191
  62.3 1.1 copy-start.14
  62.5 1.9 copy-start.15
  93.5 1.3 copy-start.4
  113.6 1.3 copy-start.2
  114.9 1.2 copy-start.8
  134.6 1.3 copy-start.1
  136.0 1.2 copy-start.10
  157.6 1.3 copy-start.3
  159.0 1.2 copy-start.6
  195.3 47.9 %reduce-scatter.6.cloned.1.call-start = ((), (), s32[]{:S(2)}) async-start(), calls=%async_computation.8 | async-start | bytes 1638400 | tf_op jit(solution)/shard_map/reduce_scatter | solution.py:180
  195.8 79.7 %reduce-scatter.8.cloned.1.call-start = ((), (), s32[]{:S(2)}) async-start(), calls=%async_computation.9 | async-start | bytes 1638400 | tf_op jit(solution)/shard_map/reduce_scatter | solution.py:180
  196.6 111.4 %reduce-scatter.12.cloned.1.call-start = ((), (), s32[]{:S(2)}) async-start(), calls=%async_computation.11 | async-start | bytes 1638400 | tf_op jit(solution)/shard_map/reduce_scatter | solution.py:180
  197.3 143.1 %reduce-scatter.10.cloned.1.call-start = ((), (), s32[]{:S(2)}) async-start(), calls=%async_computation.10 | async-start | bytes 1638400 | tf_op jit(solution)/shard_map/reduce_scatter | solution.py:180
  198.1 159.4 %all-gather.19.cloned.1.call-start = ((), (), s32[]{:S(2)}) async-start(), calls=%async_computation.17 | async-start | bytes 1310720 | tf_op jit(solution)/shard_map/all_gather | solution.py:192
  (4 other events, 4.1 us)
Sparse Core Ops, SparseCore 0:
  10.2 35.3 all-gather.10
  47.7 42.9 all-gather.12
  92.3 30.9 all-gather.14
  125.3 32.3 all-gather.16
  195.4 13.5 reduce-scatter.13
  211.9 31.2 reduce-scatter.5
  245.5 29.9 reduce-scatter.7
  278.0 29.9 reduce-scatter.11
  310.4 29.9 reduce-scatter.9
  342.0 15.5 all-gather.18

commit v2 on v1

v2 whole, which is shorter than its diff:
```python
import functools

import jax
import jax.numpy as jnp
from jax import lax
from jax.experimental import pallas as pl
from jax.experimental.pallas import tpu as pltpu
from jax.sharding import PartitionSpec as P

HEADS = 4
HEAD_DIM = 32
TOKENS = 1024
SCALE = HEAD_DIM ** (-0.5)
LOG2E = 1.4426950408889634
NEG = -1000000000.0


def contract(left, right, left_dim, right_dim):
    return lax.dot_general(
        left, right, (((left_dim,), (right_dim,)), ((), ())), preferred_element_type=jnp.float32
    )


def attention_kernel(count_ref, in_ref, bias_ref, out_ref, grad_out_ref, s_ref, dk_ref, dv_ref, grad_ref):
    cols, _, _, width = in_ref.shape
    per = bias_ref.shape[3] // width
    d = HEAD_DIM
    row, col = pl.program_id(0), pl.program_id(1)
    side = col // per
    lanes = pl.ds(pl.multiple_of((col % per) * width, width), width)

    @pl.when((row == 0) & (col == 0))
    def _():
        grad_ref[...] = jnp.zeros_like(grad_ref)

    @pl.when(col == 0)
    def _():
        dk_ref[...] = jnp.zeros_like(dk_ref)
        dv_ref[...] = jnp.zeros_like(dv_ref)

    def key(b):
        return in_ref[b, 0, d:2 * d, :]

    def value(b):
        return in_ref[b, 0, 2 * d:3 * d, :]

    def variant(live_blocks):
        q = in_ref[col, 0, 0:d, :]
        out_grad = in_ref[col, 0, 3 * d:4 * d, :]
        top = None
        for b in range(live_blocks):
            s = contract(key(b), q, 0, 0) * (SCALE * LOG2E) + bias_ref[side, b, :, lanes]
            s_ref[b] = s
            block_top = jnp.max(s, axis=0, keepdims=True)
            top = block_top if top is None else jnp.maximum(top, block_top)
        total = jnp.zeros_like(top)
        for b in range(live_blocks):
            p = jnp.exp2(s_ref[b] - top)
            s_ref[b] = p
            total = total + jnp.sum(p, axis=0, keepdims=True)
        inverse = 1.0 / total
        attended = jnp.zeros(q.shape, jnp.float32)
        for b in range(live_blocks):
            p = s_ref[b] * inverse
            s_ref[b] = p
            pb = p.astype(jnp.bfloat16)
            attended = attended + contract(value(b), pb, 1, 0)
            dv_ref[b] += contract(out_grad, pb, 1, 1)
        out_ref[col, 0, 3 * d:4 * d, :] = attended.astype(jnp.bfloat16)
        delta = jnp.sum(out_grad.astype(jnp.float32) * attended, axis=0, keepdims=True)
        dq = jnp.zeros(q.shape, jnp.float32)
        for b in range(live_blocks):
            dp = contract(value(b), out_grad, 0, 0)
            ds = s_ref[b] * (dp - delta)
            grad_ref[side, b, :, lanes] += ds
            dsb = ds.astype(jnp.bfloat16)
            dq = dq + contract(key(b), dsb, 1, 0)
            dk_ref[b] += contract(q, dsb, 1, 1)
        out_ref[col, 0, 0:d, :] = (dq * SCALE).astype(jnp.bfloat16)

    count = count_ref[0]
    for live in range(1, cols + 1):

        @pl.when((count > (live - 1) * width) & (count <= live * width))
        def _(live=live):
            variant(live)

    @pl.when(col == cols - 1)
    def _():
        for b in range(cols):
            out_ref[b, 0, d:2 * d, :] = (dk_ref[b] * SCALE).astype(jnp.bfloat16)
            out_ref[b, 0, 2 * d:3 * d, :] = dv_ref[b].astype(jnp.bfloat16)

    @pl.when((col == cols - 1) & (row == pl.num_programs(0) - 1))
    def _():
        grad_out_ref[...] = grad_ref[...].astype(jnp.bfloat16)


def attention_rows(count, packed, bias):
    cols, rows, depth, width = packed.shape
    d = HEAD_DIM
    tokens = cols * width
    packed_spec = pl.BlockSpec((cols, 1, depth, width), lambda i, j: (0, i, 0, 0))
    bias_spec = pl.BlockSpec(bias.shape, lambda i, j: (0, 0, 0, 0))
    return pl.pallas_call(
        attention_kernel,
        grid=(rows, cols),
        in_specs=[pl.BlockSpec(memory_space=pltpu.SMEM), packed_spec, bias_spec],
        out_specs=[packed_spec, bias_spec],
        out_shape=[
            jax.ShapeDtypeStruct(packed.shape, jnp.bfloat16),
            jax.ShapeDtypeStruct(bias.shape, jnp.bfloat16),
        ],
        scratch_shapes=[
            pltpu.VMEM((cols, width, width), jnp.float32),
            pltpu.VMEM((cols, d, width), jnp.float32),
            pltpu.VMEM((cols, d, width), jnp.float32),
            pltpu.VMEM(bias.shape, jnp.float32),
        ],
        compiler_params=pltpu.CompilerParams(vmem_limit_bytes=40 * 1024 * 1024),
        cost_estimate=pl.CostEstimate(
            flops=12 * rows * d * tokens * tokens,
            bytes_accessed=4 * packed.size + 6 * bias.size,
            transcendentals=rows * tokens * tokens,
        ),
    )(count, packed, bias)


def body(
    queries,
    key_vectors,
    value_vectors,
    gate_logits,
    cotangent,
    pair_normed,
    bias_weight,
    chain_lengths,
):
    rows_here = queries.shape[2]
    channels_here, row_block, col_block = pair_normed.shape
    row_count = lax.axis_size("row")
    col_count = lax.axis_size("col")
    count = jnp.sum(chain_lengths).reshape(1)

    flat_pair = pair_normed.reshape(channels_here, row_block * col_block)
    partial = jnp.dot(bias_weight.T, flat_pair, preferred_element_type=jnp.float32)
    partial = partial.astype(jnp.float16).reshape(HEADS, row_block, col_block)
    parts = lax.all_to_all(partial, "head", split_axis=0, concat_axis=0, tiled=True)
    own_bias = jnp.sum(parts.astype(jnp.float32), axis=0).T.astype(jnp.float16)
    whole = lax.all_gather(own_bias, ("row", "col"), axis=0, tiled=False)
    whole = whole.reshape(row_count, col_count, col_block, row_block)
    position = (
        jnp.arange(col_count, dtype=jnp.int32)[:, None] * col_block
        + jnp.arange(col_block, dtype=jnp.int32)[None, :]
    )
    live = (position < count[0])[None, :, :, None]
    bias = jnp.where(live, whole.astype(jnp.float32) * LOG2E, NEG)

    gate = jax.nn.sigmoid(gate_logits.astype(jnp.float32))
    cot = cotangent.astype(jnp.float32)
    out_grad = (cot * gate).astype(jnp.bfloat16)
    packed = jnp.concatenate(
        [item[0].transpose(1, 0, 2) for item in (queries, key_vectors, value_vectors, out_grad)],
        axis=1,
    )
    packed = packed.reshape(col_count, rows_here // col_count, 4 * HEAD_DIM, col_block)
    packed = lax.all_to_all(packed, "col", split_axis=0, concat_axis=0, tiled=True)

    grads, square = attention_rows(count, packed, bias)

    grads = lax.all_to_all(grads, "col", split_axis=0, concat_axis=0, tiled=True)
    grads = grads.reshape(rows_here, 4, HEAD_DIM, col_block).transpose(1, 2, 0, 3)
    query_grad, key_grad, value_grad = grads[0:1], grads[1:2], grads[2:3]
    attended = grads[3:4].astype(jnp.float32)
    gate_grad = (cot * attended * gate * (1.0 - gate)).astype(jnp.bfloat16)

    square = square.reshape(row_count * col_count, col_block, row_block)
    own_grad = lax.psum_scatter(square, ("row", "col"), scatter_dimension=0, tiled=False).T
    every_head = lax.all_gather(own_grad, "head", axis=0, tiled=False)
    pair_grad = jnp.dot(
        bias_weight,
        every_head.reshape(HEADS, row_block * col_block),
        preferred_element_type=jnp.float32,
    )
    pair_grad = pair_grad.reshape(channels_here, row_block, col_block).astype(jnp.bfloat16)
    return (query_grad, key_grad, value_grad, gate_grad, pair_grad)


def solution(mesh):
    in_specs = (
        P("head", None, "row", "col"),
        P("head", None, "row", "col"),
        P("head", None, "row", "col"),
        P("head", None, "row", "col"),
        P("head", None, "row", "col"),
        P("head", "row", "col"),
        P("head", None),
        P(),
    )
    out_specs = (
        P("head", None, "row", "col"),
        P("head", None, "row", "col"),
        P("head", None, "row", "col"),
        P("head", None, "row", "col"),
        P("head", "row", "col"),
    )
    return jax.shard_map(body, mesh=mesh, in_specs=in_specs, out_specs=out_specs, check_vma=False)
```

time: 380 us -> 372 us (0.979); the launches traced: 381 us -> 377 us
  waiting for transfers between devices: 196 us -> 118 us
  blocking collectives: 26.4 us -> 97.6 us
  other arithmetic: 6.84 us -> 13.5 us
  Pallas kernels: 70.4 us -> 66.5 us
    all_gather x1, blocking collectives: 9.19 us -> 97.6 us  [body(): whole = lax.all_gather(own_bias, ('row', 'col'), axis=0, tiled=False)]
    reduce_scatter x5 -> x1, waiting for transfers between devices: 140 us -> 95.1 us  [body(): lax.psum_scatter(square, ('row', 'col'), scatter_dimension=0, tiled=False)]
    all_to_all x1 -> x2, waiting for transfers between devices: 23.3 us -> 0.01 us  [the longest x1 0.01 us: body(): lax.all_to_all(packed, 'col', split_axis=0, concat_axis=0, tiled=True)]
    all_to_all x1 -> x0, blocking collectives: 17.2 us -> none  [body(): lax.all_to_all(square, 'col', split_axis=1, concat_axis=0, tiled=True)]
    unnamed x42 -> x19, local copies, waits for them, and re-layouts: 40.8 us -> 26.3 us
    reshape x0 -> x2, local copies, waits for them, and re-layouts: none -> 5.43 us  [the longest x1 3.91 us: body(): square = square.reshape(row_count * col_count, col_block, row_block)]
    unnamed x10 -> x2, waiting for transfers between devices: 4.35 us -> 0.03 us
    mul x1, local copies, waits for them, and re-layouts: 1.31 us -> 5.36 us  [body(): bias = jnp.where(live, whole.astype(jnp.float32) * LOG2E, NEG)]
  transfers between devices with their start and end apart: 12 -> 5, of which waited for: 9 -> 3; matrix products, arithmetic and copies ran while one was open for 8% -> 6% of each run, Pallas kernels for 14% -> 0%
where the time goes in v2:
time: 372 us; the launch traced here: 377 us
  waiting for transfers between devices  118 us (32%)
  blocking collectives  97.6 us (26%)
  Pallas kernels  66.5 us (18%)
  local copies, waits for them, and re-layouts  42.5 us (11%)
  between operations  14.1 us (4%)
  starting transfers between devices  13.7 us (4%)
  other arithmetic  13.5 us (4%)
  matrix products  10.2 us (3%)
    all_gather x1, blocking collectives, body(): whole = lax.all_gather(own_bias, ('row', 'col'), axis=0, tiled=False)  97.6 us
    reduce_scatter x1, waiting for transfers between devices, body(): lax.psum_scatter(square, ('row', 'col'), scatter_dimension=0, tiled=False)  95.1 us
    pallas_call x1, Pallas kernels, attention_rows(): pl.pallas_call(attention_kernel, grid=(rows, cols), in_specs=[pl.BlockSpe...  66.5 us
    unnamed x19, local copies, waits for them, and re-layouts  26.3 us
    all_gather x1, waiting for transfers between devices, body(): every_head = lax.all_gather(own_grad, 'head', axis=0, tiled=False)  13.1 us
    all_to_all x1, waiting for transfers between devices, body(): lax.all_to_all(partial, 'head', split_axis=0, concat_axis=0, tiled=True)  10.2 us
  transfers between devices with their start and end apart: 5, of which 3 were waited for; matrix products, arithmetic and copies ran while one was open for 6% of the time, Pallas kernels for 0%

profile of v2, /device:TPU:0, one launch (start us, length us, event | category | flops | bytes accessed | tf_op | source)
XLA Modules:
  0.0 376.6 jit_solution(2659705615631307830)
XLA Ops:
  7.2 11.6 %copy.22 = bf16[4,8,512,256]{3,1,2,0:T(8,128)(2,1)} copy(bf16[4,8,512,256]{3,2,1,0:T(8,128)(2,1)} %bitcast.47) | data formatting | bytes 16777216
  18.8 4.6 %convolution_convert_fusion.1 = f16[4,131072]{1,0:T(4,128)(2,1)S(1)} fusion(bf16[32,4]{0,1:T(4,128)(2,1)S(1)} %copy-done, bf16[32,131072]{1,0:T(8,128)(2,1)} %bitcast.41), kind=kOutput, calls=%fused_computation.1 | convolution fusion | flops 34078720 | bytes 9437440 | tf_op jit(solution)/shard_map/dot_general | solution.py:146
  24.7 4.2 %all-to-all-start.1 = ((f16[4,512,256]{2,1,0:T(8,128)(2,1)}), f16[4,512,256]{2,1,0:T(8,128)(2,1)S(1)}, u32[]{:S(2)}, u32[]{:S(2)}) async-start(f16[4,512,256]{2,1,0:T(8,128)(2,1)} %bitcast.38), calls=%async_computation.1 | async-start | bytes 2097152 | tf_op jit(solution)/shard_map/all_to_all | solution.py:148
  29.3 1.8 pad_maximum_fusion
  31.1 2.1 copy.18
  33.2 10.2 %all-to-all-done.1 = f16[4,512,256]{2,1,0:T(8,128)(2,1)S(1)} async-done(((f16[4,512,256]{2,1,0:T(8,128)(2,1)}), f16[4,512,256]{2,1,0:T(8,128)(2,1)S(1)}, u32[]{:S(2)}, u32[]{:S(2)}) %all-to-all-start.1) | async-done | bytes 1048608 | tf_op jit(solution)/shard_map/all_to_all | solution.py:148
  44.4 5.6 %all-to-all-start = ((bf16[4,10,128,256]{3,2,1,0:T(8,128)(2,1)}), bf16[4,10,128,256]{3,2,1,0:T(8,128)(2,1)S(1)}, u32[]{:S(2)}, u32[]{:S(2)}) async-start(bf16[4,10,128,256]{3,2,1,0:T(8,128)(2,1)} %bitcast.43), calls=%async_computation | async-start | bytes 5242880 | tf_op jit(solution)/shard_map/all_to_all | solution.py:167
  51.3 1.4 convert_reduce_fusion
  52.8 97.6 %all-gather.6 = f16[2048,512]{0,1:T(8,128)(2,1)S(1)} all-gather(f16[256,512]{0,1:T(8,128)(2,1)S(1)} %convert_bitcast_fusion), channel_id=2, replica_groups=mesh['row'=2,'col'=4,'head'=4] {'row','col'}, dimensions={0}, use_global_device_ids=true | all-gather | bytes 2359296 | tf_op jit(solution)/shard_map/all_gather | solution.py:150
  150.4 2.6 convert_multiply_fusion
  153.0 5.4 %copy.19 = f32[2048,512]{1,0:T(8,128)} copy(f32[2048,512]{0,1:T(8,128)} %convert_multiply_fusion) | data formatting | bytes 8388608 | tf_op jit(solution)/shard_map/mul | solution.py:157
  158.3 4.6 %broadcast_select_fusion.bias_ref = f32[2,4,256,512]{3,2,1,0:T(8,128)} fusion(f32[2,4,256,512]{3,2,1,0:T(8,128)} %bitcast.42, pred[4,256]{1,0:T(4,128)(4,1)S(1)} %add_compare_fusion), kind=kLoop, calls=%fused_computation.5 | loop fusion | flops 1048576 | bytes 8389632 | tf_op jit(solution)/shard_map/jit(_where)/select_n | solution.py:157
  163.0 2.2 copy-done.1
  165.2 66.5 %shard_map.119 = (bf16[4,10,128,256]{3,2,1,0:T(8,128)(2,1)}, bf16[2,4,256,512]{3,2,1,0:T(8,128)(2,1)S(1)}) custom-call(s32[1]{0:T(128)} %bitcast.count_ref, bf16[4,10,128,256]{3,2,1,0:T(8,128)(2,1)S(1)} %all-to-all-done.in_ref, f32[2,4,256,512]{3,2,1,0:T(8,128)S(1)} %copy-done.1), custom_call_target="tpu_custom_call" | custom-call | flops 4026531840 | bytes 11534336 | tf_op jit(solution)/shard_map/pallas_call | solution.py:105
  233.0 3.9 %copy.21 = bf16[8,256,512]{1,2,0:T(8,128)(2,1)} copy(bf16[8,256,512]{2,1,0:T(8,128)(2,1)} %bitcast.39) | data formatting | bytes 4194304 | tf_op jit(solution)/shard_map/reshape | solution.py:177
  236.9 3.7 all-to-all-start.2
  240.9 95.1 %reduce-scatter.2.cloned.1.call-done = bf16[1,256,512]{1,2,0:T(8,128)(2,1)} async-done(((bf16[8,256,512]{1,2,0:T(8,128)(2,1)}), bf16[1,256,512]{1,2,0:T(8,128)(2,1)}) %reduce-scatter.2.cloned.1.call-update) | async-done | bytes 262160 | tf_op jit(solution)/shard_map/reduce_scatter | solution.py:178
  336.0 1.5 copy.27
  337.5 1.3 fusion.5
  338.9 1.3 fusion.3
  340.2 13.1 %all-gather.5.cloned.1.call-done = bf16[2048,256]{1,0:T(8,128)(2,1)} async-done(((bf16[512,256]{1,0:T(8,128)(2,1)}), bf16[2048,256]{1,0:T(8,128)(2,1)}) %all-gather.5.cloned.1.call-update) | async-done | bytes 1048592 | tf_op jit(solution)/shard_map/all_gather | solution.py:179
  353.4 2.0 reshape.71
  355.4 5.6 %convolution_convert_fusion = bf16[131072,32]{0,1:T(8,128)(2,1)} fusion(bf16[4,131072]{1,0:T(4,128)(2,1)S(1)} %reshape.71, bf16[32,4]{0,1:T(4,128)(2,1)S(1)} %copy-done), kind=kOutput, calls=%fused_computation | convolution fusion | flops 37748736 | bytes 9437440 | tf_op jit(solution)/shard_map/dot_general | solution.py:180
  361.0 8.8 %copy.24 = bf16[4,8,512,256]{3,2,1,0:T(8,128)(2,1)} copy(bf16[4,8,512,256]{3,1,2,0:T(8,128)(2,1)} %bitcast.40) | data formatting | bytes 16777216
  (27 shorter events, 5.7 us)
Async XLA Ops:
  7.2 11.7 %copy-start = (bf16[32,4]{0,1:T(4,128)(2,1)S(1)}, bf16[32,4]{0,1:T(4,128)(2,1)}, u32[]{:S(2)}) copy-start(bf16[32,4]{0,1:T(4,128)(2,1)} %param.14) | copy-start | bytes 772
  23.4 5.5 %copy-start.4 = (bf16[1,32,40,256]{3,2,1,0:T(8,128)(2,1)S(1)}, bf16[1,32,40,256]{3,2,1,0:T(8,128)(2,1)}, u32[]{:S(2)}) copy-start(bf16[1,32,40,256]{3,2,1,0:T(8,128)(2,1)} %param.12) | copy-start | bytes 1966084
  23.4 5.5 %copy-start.5 = (bf16[1,32,40,256]{3,2,1,0:T(8,128)(2,1)S(1)}, bf16[1,32,40,256]{3,2,1,0:T(8,128)(2,1)}, u32[]{:S(2)}) copy-start(bf16[1,32,40,256]{3,2,1,0:T(8,128)(2,1)} %param.11) | copy-start | bytes 1966084
  24.7 18.7 %all-to-all-start.1 = ((f16[4,512,256]{2,1,0:T(8,128)(2,1)}), f16[4,512,256]{2,1,0:T(8,128)(2,1)S(1)}, u32[]{:S(2)}, u32[]{:S(2)}) async-start(f16[4,512,256]{2,1,0:T(8,128)(2,1)} %bitcast.38), calls=%async_computation.1 | async-start | bytes 2097152 | tf_op jit(solution)/shard_map/all_to_all | solution.py:148
  43.4 1.0 copy-start.3
  43.4 6.5 %copy-start.7 = (s32[8]{0:T(128)S(1)}, s32[8]{0:T(128)}, u32[]{:S(2)}) copy-start(s32[8]{0:T(128)} %param.15) | copy-start | bytes 100
  44.4 118.6 %all-to-all-start = ((bf16[4,10,128,256]{3,2,1,0:T(8,128)(2,1)}), bf16[4,10,128,256]{3,2,1,0:T(8,128)(2,1)S(1)}, u32[]{:S(2)}, u32[]{:S(2)}) async-start(bf16[4,10,128,256]{3,2,1,0:T(8,128)(2,1)} %bitcast.43), calls=%async_computation | async-start | bytes 5242880 | tf_op jit(solution)/shard_map/all_to_all | solution.py:167
  49.9 286.0 %reduce-scatter.2.cloned.1.call-start = ((), (), s32[]{:S(2)}) async-start(), calls=%async_computation.4 | async-start | bytes 2359296 | tf_op jit(solution)/shard_map/reduce_scatter | solution.py:178
  163.0 2.2 copy-start.1
  231.7 1.3 copy-start.2
  236.9 99.1 %all-to-all-start.2 = ((bf16[4,10,128,256]{3,2,1,0:T(8,128)(2,1)}), bf16[4,10,128,256]{3,2,1,0:T(8,128)(2,1)S(1)}, u32[]{:S(2)}, u32[]{:S(2)}) async-start(bf16[4,10,128,256]{3,2,1,0:T(8,128)(2,1)} %get-tuple-element.7), calls=%async_computation.2 | async-start | bytes 5242880 | tf_op jit(solution)/shard_map/all_to_all | solution.py:171
  240.6 112.8 %all-gather.5.cloned.1.call-start = ((), (), s32[]{:S(2)}) async-start(), calls=%async_computation.5 | async-start | bytes 1310720 | tf_op jit(solution)/shard_map/all_gather | solution.py:179
  337.5 1.4 copy-start.6
Sparse Core Ops, SparseCore 0:
  237.0 98.8 reduce-scatter.1
  337.5 15.8 all-gather.4

commit v3 on v2

--- a/solution.py
+++ b/solution.py
@@ -11,6 +11,9 @@
 HEAD_DIM = 32
 TOKENS = 1024
 SCALE = HEAD_DIM ** (-0.5)
+SUB = 16
+ROW_TILE = 64
+PAIR_HERE = 32
 LOG2E = 1.4426950408889634
 NEG = -1000000000.0
 
@@ -126,6 +129,61 @@
     )(count, packed, bias)
 
 
+def project_kernel(weight_ref, pair_ref, out_ref):
+    channels, rows, _ = pair_ref.shape
+
+    def step(i, carry):
+        part = pl.ds(pl.multiple_of(i * SUB, SUB), SUB)
+        sums = [None] * HEADS
+        for c in range(channels):
+            x = pair_ref[c, part, :].astype(jnp.float32)
+            for h in range(HEADS):
+                term = x * weight_ref[c * HEADS + h]
+                sums[h] = term if sums[h] is None else sums[h] + term
+        for h in range(HEADS):
+            out_ref[h, part, :] = sums[h]
+        return carry
+
+    lax.fori_loop(0, rows // SUB, step, 0)
+
+
+def expand_kernel(weight_ref, grad_ref, out_ref):
+    channels, rows, _ = out_ref.shape
+
+    def step(i, carry):
+        part = pl.ds(pl.multiple_of(i * SUB, SUB), SUB)
+        heads = [grad_ref[h, part, :].astype(jnp.float32) for h in range(HEADS)]
+        for c in range(channels):
+            total = heads[0] * weight_ref[c * HEADS]
+            for h in range(1, HEADS):
+                total = total + heads[h] * weight_ref[c * HEADS + h]
+            out_ref[c, part, :] = total.astype(jnp.bfloat16)
+        return carry
+
+    lax.fori_loop(0, rows // SUB, step, 0)
+
+
+def pair_call(kernel, weight, source, leading, dtype):
+    _, rows, width = source.shape
+    tile = min(ROW_TILE, rows)
+    return pl.pallas_call(
+        kernel,
+        grid=(rows // tile,),
+        in_specs=[
+            pl.BlockSpec(memory_space=pltpu.SMEM),
+            pl.BlockSpec((source.shape[0], tile, width), lambda i: (0, i, 0)),
+        ],
+        out_specs=pl.BlockSpec((leading, tile, width), lambda i: (0, i, 0)),
+        out_shape=jax.ShapeDtypeStruct((leading, rows, width), dtype),
+        compiler_params=pltpu.CompilerParams(vmem_limit_bytes=40 * 1024 * 1024),
+        cost_estimate=pl.CostEstimate(
+            flops=2 * HEADS * PAIR_HERE * rows * width,
+            bytes_accessed=(2 * PAIR_HERE + 4 * HEADS) * rows * width,
+            transcendentals=0,
+        ),
+    )(weight, source)
+
+
 def body(
     queries,
     key_vectors,
@@ -142,12 +200,13 @@
     col_count = lax.axis_size("col")
     count = jnp.sum(chain_lengths).reshape(1)
 
-    flat_pair = pair_normed.reshape(channels_here, row_block * col_block)
-    partial = jnp.dot(bias_weight.T, flat_pair, preferred_element_type=jnp.float32)
-    partial = partial.astype(jnp.float16).reshape(HEADS, row_block, col_block)
+    weight = bias_weight.astype(jnp.float32).reshape(-1)
+    partial = pair_call(project_kernel, weight, pair_normed, HEADS, jnp.float32)
+    partial = partial.astype(jnp.float16)
     parts = lax.all_to_all(partial, "head", split_axis=0, concat_axis=0, tiled=True)
     own_bias = jnp.sum(parts.astype(jnp.float32), axis=0).T.astype(jnp.float16)
-    whole = lax.all_gather(own_bias, ("row", "col"), axis=0, tiled=False)
+    line = lax.all_gather(own_bias, "col", axis=0, tiled=True)
+    whole = lax.all_gather(line, "row", axis=0, tiled=True)
     whole = whole.reshape(row_count, col_count, col_block, row_block)
     position = (
         jnp.arange(col_count, dtype=jnp.int32)[:, None] * col_block
@@ -174,15 +233,11 @@
     attended = grads[3:4].astype(jnp.float32)
     gate_grad = (cot * attended * gate * (1.0 - gate)).astype(jnp.bfloat16)
 
-    square = square.reshape(row_count * col_count, col_block, row_block)
-    own_grad = lax.psum_scatter(square, ("row", "col"), scatter_dimension=0, tiled=False).T
+    square = square.reshape(row_count * col_count * col_block, row_block)
+    line_grad = lax.psum_scatter(square, "row", scatter_dimension=0, tiled=True)
+    own_grad = lax.psum_scatter(line_grad, "col", scatter_dimension=0, tiled=True).T
     every_head = lax.all_gather(own_grad, "head", axis=0, tiled=False)
-    pair_grad = jnp.dot(
-        bias_weight,
-        every_head.reshape(HEADS, row_block * col_block),
-        preferred_element_type=jnp.float32,
-    )
-    pair_grad = pair_grad.reshape(channels_here, row_block, col_block).astype(jnp.bfloat16)
+    pair_grad = pair_call(expand_kernel, weight, every_head, channels_here, jnp.bfloat16)
     return (query_grad, key_grad, value_grad, gate_grad, pair_grad)
 
 

time: 372 us -> 324 us (0.87); the launches traced: 377 us -> 324 us
  waiting for transfers between devices: 118 us -> 91 us
  local copies, waits for them, and re-layouts: 42.5 us -> 24.4 us
  matrix products: 10.2 us -> 0 us
    reduce_scatter x1 -> x2, waiting for transfers between devices: 95.1 us -> 66.9 us  [the longest x1 40.2 us: body(): lax.psum_scatter(line_grad, 'col', scatter_dimension=0, tiled=True)]
    unnamed x19 -> x18, local copies, waits for them, and re-layouts: 26.3 us -> 9.24 us
    pallas_call x0 -> x2, Pallas kernels: none -> 14.9 us  [pair_call(): pl.pallas_call(kernel, grid=(rows // tile,), in_specs=[pl.BlockSpec(memor...]
    pallas_call x1, Pallas kernels: 66.5 us -> 55.1 us  [attention_rows(): pl.pallas_call(attention_kernel, grid=(rows, cols), in_specs=[pl.BlockSpe...]
    dot_general x2 -> x0, matrix products: 10.2 us -> none  [the longest x1 5.59 us: body(): jnp.dot(bias_weight, every_head.reshape(HEADS, row_block * col_block), pr...]
    all_to_all x1, waiting for transfers between devices: 0.01 us -> 6 us  [body(): lax.all_to_all(grads, 'col', split_axis=0, concat_axis=0, tiled=True)]
    all_gather x1, waiting for transfers between devices: 13.1 us -> 7.79 us  [body(): every_head = lax.all_gather(own_grad, 'head', axis=0, tiled=False)]
    all_gather x1 -> x2, blocking collectives: 97.6 us -> 96.2 us  [the longest x1 73.2 us: body(): line = lax.all_gather(own_bias, 'col', axis=0, tiled=True)]
  transfers between devices with their start and end apart: 5 -> 6, of which waited for: 3 -> 5; matrix products, arithmetic and copies ran while one was open for 6% -> 7% of each run, Pallas kernels for 0% -> 0%
where the time goes in v3:
time: 324 us
  blocking collectives  96.2 us (30%)
  waiting for transfers between devices  91 us (28%)
  Pallas kernels  70.1 us (22%)
  local copies, waits for them, and re-layouts  24.4 us (8%)
  other arithmetic  14.7 us (5%)
  between operations  13.8 us (4%)
  starting transfers between devices  13.6 us (4%)
    all_gather x1, blocking collectives, body(): line = lax.all_gather(own_bias, 'col', axis=0, tiled=True)  73.2 us
    pallas_call x1, Pallas kernels, attention_rows(): pl.pallas_call(attention_kernel, grid=(rows, cols), in_specs=[pl.BlockSpe...  55.1 us
    reduce_scatter x1, waiting for transfers between devices, body(): lax.psum_scatter(line_grad, 'col', scatter_dimension=0, tiled=True)  40.2 us
    reduce_scatter x1, waiting for transfers between devices, body(): line_grad = lax.psum_scatter(square, 'row', scatter_dimension=0, tiled=True)  26.7 us
    all_gather x1, blocking collectives, body(): whole = lax.all_gather(line, 'row', axis=0, tiled=True)  22.9 us
    pallas_call x2, Pallas kernels, pair_call(): pl.pallas_call(kernel, grid=(rows // tile,), in_specs=[pl.BlockSpec(memor...  14.9 us
    all_to_all x1, waiting for transfers between devices, body(): lax.all_to_all(partial, 'head', split_axis=0, concat_axis=0, tiled=True)  10.2 us
    unnamed x18, local copies, waits for them, and re-layouts  9.24 us
  transfers between devices with their start and end apart: 6, of which 5 were waited for; matrix products, arithmetic and copies ran while one was open for 7% of the time, Pallas kernels for 0%

profile of v3, /device:TPU:0, one launch (start us, length us, event | category | flops | bytes accessed | tf_op | source)
XLA Modules:
  0.0 323.7 jit_solution(14339682942122499060)
XLA Ops:
  8.1 3.4 %copy-done = bf16[32,512,256]{2,1,0:T(8,128)(2,1)S(1)} copy-done((bf16[32,512,256]{2,1,0:T(8,128)(2,1)S(1)}, bf16[32,512,256]{2,1,0:T(8,128)(2,1)}, u32[]{:S(2)}) %copy-start) | copy-done | bytes 8388632
  11.4 7.4 %shard_map.119 = f32[4,512,256]{2,1,0:T(8,128)S(1)} custom-call(f32[128]{0:T(128)S(1)} %reshape.66.weight_ref, bf16[32,512,256]{2,1,0:T(8,128)(2,1)S(1)} %copy-done), custom_call_target="tpu_custom_call" | custom-call | flops 33554432 | bytes 10485760 | tf_op jit(solution)/shard_map/pallas_call | solution.py:169
  20.0 4.2 %all-to-all-start.1 = ((f16[4,512,256]{2,1,0:T(8,128)(2,1)}), f16[4,512,256]{2,1,0:T(8,128)(2,1)S(1)}, u32[]{:S(2)}, u32[]{:S(2)}) async-start(f16[4,512,256]{2,1,0:T(8,128)(2,1)} %convert_element_type.35), calls=%async_computation.1 | async-start | bytes 2097152 | tf_op jit(solution)/shard_map/all_to_all | solution.py:206
  24.6 1.8 pad_maximum_fusion
  26.4 2.1 copy.21
  28.5 10.2 %all-to-all-done.1 = f16[4,512,256]{2,1,0:T(8,128)(2,1)S(1)} async-done(((f16[4,512,256]{2,1,0:T(8,128)(2,1)}), f16[4,512,256]{2,1,0:T(8,128)(2,1)S(1)}, u32[]{:S(2)}, u32[]{:S(2)}) %all-to-all-start.1) | async-done | bytes 1048608 | tf_op jit(solution)/shard_map/all_to_all | solution.py:206
  39.7 5.6 %all-to-all-start = ((bf16[4,10,128,256]{3,2,1,0:T(8,128)(2,1)}), bf16[4,10,128,256]{3,2,1,0:T(8,128)(2,1)S(1)}, u32[]{:S(2)}, u32[]{:S(2)}) async-start(bf16[4,10,128,256]{3,2,1,0:T(8,128)(2,1)} %bitcast.29), calls=%async_computation | async-start | bytes 5242880 | tf_op jit(solution)/shard_map/all_to_all | solution.py:226
  46.6 1.4 convert_reduce_fusion
  48.1 73.2 %all-gather.6 = f16[1024,512]{0,1:T(8,128)(2,1)S(1)} all-gather(f16[256,512]{0,1:T(8,128)(2,1)S(1)} %convert_bitcast_fusion), channel_id=1, replica_groups=mesh['row'=2,'col'=4,'head'=4] {'col'}, dimensions={0}, use_global_device_ids=true | all-gather | bytes 1310720 | tf_op jit(solution)/shard_map/all_gather | solution.py:208
  121.4 22.9 %all-gather.7 = f16[2048,512]{0,1:T(8,128)(2,1)S(1)} all-gather(f16[1024,512]{0,1:T(8,128)(2,1)S(1)} %all-gather.6), channel_id=1, replica_groups=mesh['row'=2,'col'=4,'head'=4] {'row'}, dimensions={0}, use_global_device_ids=true | all-gather | bytes 3145728 | tf_op jit(solution)/shard_map/all_gather | solution.py:209
  144.3 2.6 convert_multiply_fusion
  146.9 5.4 %copy.23 = f32[2048,512]{1,0:T(8,128)} copy(f32[2048,512]{0,1:T(8,128)} %convert_multiply_fusion) | data formatting | bytes 8388608 | tf_op jit(solution)/shard_map/mul | solution.py:216
  152.2 4.6 %broadcast_select_fusion.bias_ref = f32[2,4,256,512]{3,2,1,0:T(8,128)} fusion(f32[2,4,256,512]{3,2,1,0:T(8,128)} %bitcast.27, pred[4,256]{1,0:T(4,128)(4,1)S(1)} %add_compare_fusion), kind=kLoop, calls=%fused_computation.3 | loop fusion | flops 1048576 | bytes 8389632 | tf_op jit(solution)/shard_map/jit(_where)/select_n | solution.py:216
  156.9 2.2 copy-done.1
  159.1 55.1 %shard_map.120 = (bf16[4,10,128,256]{3,2,1,0:T(8,128)(2,1)}, bf16[2,4,256,512]{3,2,1,0:T(8,128)(2,1)S(1)}) custom-call(s32[1]{0:T(128)} %bitcast.count_ref, bf16[4,10,128,256]{3,2,1,0:T(8,128)(2,1)S(1)} %all-to-all-done.in_ref, f32[2,4,256,512]{3,2,1,0:T(8,128)S(1)} %copy-done.1), custom_call_target="tpu_custom_call" | custom-call | flops 4026531840 | bytes 11534336 | tf_op jit(solution)/shard_map/pallas_call | solution.py:108
  215.5 3.9 %copy.25 = bf16[2048,512]{0,1:T(8,128)(2,1)} copy(bf16[2048,512]{1,0:T(8,128)(2,1)} %bitcast.25) | data formatting | bytes 4194304 | tf_op jit(solution)/shard_map/reshape | solution.py:236
  219.5 3.7 %all-to-all-start.2 = ((bf16[4,10,128,256]{3,2,1,0:T(8,128)(2,1)}), bf16[4,10,128,256]{3,2,1,0:T(8,128)(2,1)S(1)}, u32[]{:S(2)}, u32[]{:S(2)}) async-start(bf16[4,10,128,256]{3,2,1,0:T(8,128)(2,1)} %get-tuple-element.7), calls=%async_computation.2 | async-start | bytes 5242880 | tf_op jit(solution)/shard_map/all_to_all | solution.py:230
  223.2 26.7 %reduce-scatter.3.cloned.1.call-done = bf16[1024,512]{0,1:T(8,128)(2,1)} async-done(((bf16[2048,512]{0,1:T(8,128)(2,1)}), bf16[1024,512]{0,1:T(8,128)(2,1)}) %reduce-scatter.3.cloned.1.call-update) | async-done | bytes 1048592 | tf_op jit(solution)/shard_map/reduce_scatter | solution.py:237
  250.0 40.2 %reduce-scatter.5.cloned.1.call-done = bf16[256,512]{0,1:T(8,128)(2,1)} async-done(((bf16[1024,512]{0,1:T(8,128)(2,1)}), bf16[256,512]{0,1:T(8,128)(2,1)}) %reduce-scatter.5.cloned.1.call-update) | async-done | bytes 262160 | tf_op jit(solution)/shard_map/reduce_scatter | solution.py:238
  290.2 6.0 %all-to-all-done.2 = bf16[4,10,128,256]{3,2,1,0:T(8,128)(2,1)S(1)} async-done(((bf16[4,10,128,256]{3,2,1,0:T(8,128)(2,1)}), bf16[4,10,128,256]{3,2,1,0:T(8,128)(2,1)S(1)}, u32[]{:S(2)}, u32[]{:S(2)}) %all-to-all-start.2) | async-done | bytes 2621472 | tf_op jit(solution)/shard_map/all_to_all | solution.py:230
  296.2 1.5 copy.27
  299.2 1.3 fusion.3
  300.6 7.8 %all-gather.5.cloned.1.call-done = bf16[2048,256]{1,0:T(8,128)(2,1)} async-done(((bf16[512,256]{1,0:T(8,128)(2,1)}), bf16[2048,256]{1,0:T(8,128)(2,1)}) %all-gather.5.cloned.1.call-update) | async-done | bytes 1048592 | tf_op jit(solution)/shard_map/all_gather | solution.py:239
  309.6 7.5 %shard_map.121 = bf16[32,512,256]{2,1,0:T(8,128)(2,1)} custom-call(f32[128]{0:T(128)S(1)} %reshape.66.weight_ref, bf16[4,512,256]{2,1,0:T(8,128)(2,1)S(1)} %bitcast.26), custom_call_target="tpu_custom_call" | custom-call | flops 33554432 | bytes 10485760 | tf_op jit(solution)/shard_map/pallas_call | solution.py:169
  (32 shorter events, 8.9 us)
Async XLA Ops:
  8.0 3.4 %copy-start = (bf16[32,512,256]{2,1,0:T(8,128)(2,1)S(1)}, bf16[32,512,256]{2,1,0:T(8,128)(2,1)}, u32[]{:S(2)}) copy-start(bf16[32,512,256]{2,1,0:T(8,128)(2,1)} %pair_ref.1) | copy-start | bytes 25165828
  18.8 5.4 %copy-start.5 = (bf16[1,32,40,256]{3,2,1,0:T(8,128)(2,1)S(1)}, bf16[1,32,40,256]{3,2,1,0:T(8,128)(2,1)}, u32[]{:S(2)}) copy-start(bf16[1,32,40,256]{3,2,1,0:T(8,128)(2,1)} %param.12) | copy-start | bytes 1966084
  18.8 5.4 %copy-start.6 = (bf16[1,32,40,256]{3,2,1,0:T(8,128)(2,1)S(1)}, bf16[1,32,40,256]{3,2,1,0:T(8,128)(2,1)}, u32[]{:S(2)}) copy-start(bf16[1,32,40,256]{3,2,1,0:T(8,128)(2,1)} %param.11) | copy-start | bytes 1966084
  20.0 18.7 %all-to-all-start.1 = ((f16[4,512,256]{2,1,0:T(8,128)(2,1)}), f16[4,512,256]{2,1,0:T(8,128)(2,1)S(1)}, u32[]{:S(2)}, u32[]{:S(2)}) async-start(f16[4,512,256]{2,1,0:T(8,128)(2,1)} %convert_element_type.35), calls=%async_computation.1 | async-start | bytes 2097152 | tf_op jit(solution)/shard_map/all_to_all | solution.py:206
  38.7 1.0 copy-start.4
  38.7 6.5 %copy-start.8 = (s32[8]{0:T(128)S(1)}, s32[8]{0:T(128)}, u32[]{:S(2)}) copy-start(s32[8]{0:T(128)} %param.15) | copy-start | bytes 100
  39.7 117.2 %all-to-all-start = ((bf16[4,10,128,256]{3,2,1,0:T(8,128)(2,1)}), bf16[4,10,128,256]{3,2,1,0:T(8,128)(2,1)S(1)}, u32[]{:S(2)}, u32[]{:S(2)}) async-start(bf16[4,10,128,256]{3,2,1,0:T(8,128)(2,1)} %bitcast.29), calls=%async_computation | async-start | bytes 5242880 | tf_op jit(solution)/shard_map/all_to_all | solution.py:226
  45.3 204.7 %reduce-scatter.3.cloned.1.call-start = ((), (), s32[]{:S(2)}) async-start(), calls=%async_computation.5 | async-start | bytes 3145728 | tf_op jit(solution)/shard_map/reduce_scatter | solution.py:237
  156.9 2.2 copy-start.1
  214.2 1.3 copy-start.2
  219.5 76.7 %all-to-all-start.2 = ((bf16[4,10,128,256]{3,2,1,0:T(8,128)(2,1)}), bf16[4,10,128,256]{3,2,1,0:T(8,128)(2,1)S(1)}, u32[]{:S(2)}, u32[]{:S(2)}) async-start(bf16[4,10,128,256]{3,2,1,0:T(8,128)(2,1)} %get-tuple-element.7), calls=%async_computation.2 | async-start | bytes 5242880 | tf_op jit(solution)/shard_map/all_to_all | solution.py:230
  223.2 67.0 %reduce-scatter.5.cloned.1.call-start = ((), (), s32[]{:S(2)}) async-start(), calls=%async_computation.6 | async-start | bytes 1310720 | tf_op jit(solution)/shard_map/reduce_scatter | solution.py:238
  250.0 58.4 %all-gather.5.cloned.1.call-start = ((), (), s32[]{:S(2)}) async-start(), calls=%async_computation.7 | async-start | bytes 1310720 | tf_op jit(solution)/shard_map/all_gather | solution.py:239
  297.8 1.5 copy-start.7
  308.4 1.2 copy-start.3
Sparse Core Ops, SparseCore 0:
  219.6 30.2 reduce-scatter.2
  252.4 37.8 reduce-scatter.4
  291.8 16.5 all-gather.4

commit v4 on v3

--- a/solution.py
+++ b/solution.py
@@ -24,8 +24,8 @@
     )
 
 
-def attention_kernel(count_ref, in_ref, bias_ref, out_ref, grad_out_ref, s_ref, dk_ref, dv_ref, grad_ref):
-    cols, _, _, width = in_ref.shape
+def attention_kernel(count_ref, qk_ref, va_ref, bias_ref, out_ref, grad_out_ref, s_ref, dk_ref, dv_ref, grad_ref):
+    cols, _, _, width = qk_ref.shape
     per = bias_ref.shape[3] // width
     d = HEAD_DIM
     row, col = pl.program_id(0), pl.program_id(1)
@@ -42,14 +42,14 @@
         dv_ref[...] = jnp.zeros_like(dv_ref)
 
     def key(b):
-        return in_ref[b, 0, d:2 * d, :]
+        return qk_ref[b, 0, d:2 * d, :]
 
     def value(b):
-        return in_ref[b, 0, 2 * d:3 * d, :]
+        return va_ref[b, 0, 0:d, :]
 
     def variant(live_blocks):
-        q = in_ref[col, 0, 0:d, :]
-        out_grad = in_ref[col, 0, 3 * d:4 * d, :]
+        q = qk_ref[col, 0, 0:d, :]
+        out_grad = va_ref[col, 0, d:2 * d, :]
         top = None
         for b in range(live_blocks):
             s = contract(key(b), q, 0, 0) * (SCALE * LOG2E) + bias_ref[side, b, :, lanes]
@@ -99,19 +99,20 @@
         grad_out_ref[...] = grad_ref[...].astype(jnp.bfloat16)
 
 
-def attention_rows(count, packed, bias):
-    cols, rows, depth, width = packed.shape
+def attention_rows(count, qk, va, bias):
+    cols, rows, depth, width = qk.shape
     d = HEAD_DIM
     tokens = cols * width
-    packed_spec = pl.BlockSpec((cols, 1, depth, width), lambda i, j: (0, i, 0, 0))
+    half_spec = pl.BlockSpec((cols, 1, depth, width), lambda i, j: (0, i, 0, 0))
+    packed_spec = pl.BlockSpec((cols, 1, 2 * depth, width), lambda i, j: (0, i, 0, 0))
     bias_spec = pl.BlockSpec(bias.shape, lambda i, j: (0, 0, 0, 0))
     return pl.pallas_call(
         attention_kernel,
         grid=(rows, cols),
-        in_specs=[pl.BlockSpec(memory_space=pltpu.SMEM), packed_spec, bias_spec],
+        in_specs=[pl.BlockSpec(memory_space=pltpu.SMEM), half_spec, half_spec, bias_spec],
         out_specs=[packed_spec, bias_spec],
         out_shape=[
-            jax.ShapeDtypeStruct(packed.shape, jnp.bfloat16),
+            jax.ShapeDtypeStruct((cols, rows, 2 * depth, width), jnp.bfloat16),
             jax.ShapeDtypeStruct(bias.shape, jnp.bfloat16),
         ],
         scratch_shapes=[
@@ -123,10 +124,10 @@
         compiler_params=pltpu.CompilerParams(vmem_limit_bytes=40 * 1024 * 1024),
         cost_estimate=pl.CostEstimate(
             flops=12 * rows * d * tokens * tokens,
-            bytes_accessed=4 * packed.size + 6 * bias.size,
+            bytes_accessed=8 * qk.size + 6 * bias.size,
             transcendentals=rows * tokens * tokens,
         ),
-    )(count, packed, bias)
+    )(count, qk, va, bias)
 
 
 def project_kernel(weight_ref, pair_ref, out_ref):
@@ -200,11 +201,33 @@
     col_count = lax.axis_size("col")
     count = jnp.sum(chain_lengths).reshape(1)
 
+    def pack(items):
+        packed = jnp.concatenate([item[0].transpose(1, 0, 2) for item in items], axis=1)
+        return packed.reshape(col_count, rows_here // col_count, 2 * HEAD_DIM, col_block)
+
+    def exchange(packed):
+        return lax.all_to_all(packed, "col", split_axis=0, concat_axis=0, tiled=True)
+
+    gate = jax.nn.sigmoid(gate_logits.astype(jnp.float32))
+    cot = cotangent.astype(jnp.float32)
+    qk = pack((queries, key_vectors))
+    qk, pair_normed = lax.optimization_barrier((qk, pair_normed))
+    qk = exchange(qk)
+
     weight = bias_weight.astype(jnp.float32).reshape(-1)
     partial = pair_call(project_kernel, weight, pair_normed, HEADS, jnp.float32)
     partial = partial.astype(jnp.float16)
-    parts = lax.all_to_all(partial, "head", split_axis=0, concat_axis=0, tiled=True)
-    own_bias = jnp.sum(parts.astype(jnp.float32), axis=0).T.astype(jnp.float16)
+    head_count = lax.axis_size("head")
+    head = lax.axis_index("head")
+    own_bias = lax.dynamic_index_in_dim(partial, head, 0, keepdims=False).astype(jnp.float32)
+    for shift in range(1, head_count):
+        sent = lax.dynamic_index_in_dim(partial, (head + shift) % head_count, 0, keepdims=False)
+        perm = [(i, (i + shift) % head_count) for i in range(head_count)]
+        own_bias = own_bias + lax.ppermute(sent, "head", perm).astype(jnp.float32)
+    own_bias = own_bias.T.astype(jnp.float16)
+    va = pack((value_vectors, (cot * gate).astype(jnp.bfloat16)))
+    own_bias, qk, va = lax.optimization_barrier((own_bias, qk, va))
+    va = exchange(va)
     line = lax.all_gather(own_bias, "col", axis=0, tiled=True)
     whole = lax.all_gather(line, "row", axis=0, tiled=True)
     whole = whole.reshape(row_count, col_count, col_block, row_block)
@@ -215,17 +238,7 @@
     live = (position < count[0])[None, :, :, None]
     bias = jnp.where(live, whole.astype(jnp.float32) * LOG2E, NEG)
 
-    gate = jax.nn.sigmoid(gate_logits.astype(jnp.float32))
-    cot = cotangent.astype(jnp.float32)
-    out_grad = (cot * gate).astype(jnp.bfloat16)
-    packed = jnp.concatenate(
-        [item[0].transpose(1, 0, 2) for item in (queries, key_vectors, value_vectors, out_grad)],
-        axis=1,
-    )
-    packed = packed.reshape(col_count, rows_here // col_count, 4 * HEAD_DIM, col_block)
-    packed = lax.all_to_all(packed, "col", split_axis=0, concat_axis=0, tiled=True)
-
-    grads, square = attention_rows(count, packed, bias)
+    grads, square = attention_rows(count, qk, va, bias)
 
     grads = lax.all_to_all(grads, "col", split_axis=0, concat_axis=0, tiled=True)
     grads = grads.reshape(rows_here, 4, HEAD_DIM, col_block).transpose(1, 2, 0, 3)

time: 324 us -> 309 us (0.954); the launches traced: 324 us -> 314 us
  blocking collectives: 96.2 us -> 69.7 us
  Pallas kernels: 70.1 us -> 82.1 us
  starting transfers between devices: 13.6 us -> 18 us
    all_gather x1, blocking collectives: 73.2 us -> 47 us  [body(): line = lax.all_gather(own_bias, 'col', axis=0, tiled=True)]
    pallas_call x1, Pallas kernels: 55.1 us -> 67.2 us  [attention_rows(): pl.pallas_call(attention_kernel, grid=(rows, cols), in_specs=[pl.BlockSpe...]
    all_to_all x2, waiting for transfers between devices: 10.2 us -> 3.35 us  [exchange(): lax.all_to_all(packed, 'col', split_axis=0, concat_axis=0, tiled=True)]
    ppermute x0 -> x3, waiting for transfers between devices: none -> 6.6 us  [body(): own_bias = own_bias + lax.ppermute(sent, 'head', perm).astype(jnp.float32)]
    ppermute x0 -> x3, starting transfers between devices: none -> 3.27 us  [body(): own_bias = own_bias + lax.ppermute(sent, 'head', perm).astype(jnp.float32)]
    unnamed x18 -> x22, local copies, waits for them, and re-layouts: 9.24 us -> 9.89 us
  transfers between devices with their start and end apart: 6 -> 9, of which waited for: 5 -> 7; matrix products, arithmetic and copies ran while one was open for 7% -> 8% of each run, Pallas kernels for 0% -> 2%
where the time goes in v4:
time: 309 us; the launch traced here: 314 us
  waiting for transfers between devices  89.1 us (29%)
  Pallas kernels  82.1 us (27%)
  blocking collectives  69.7 us (23%)
  local copies, waits for them, and re-layouts  26.1 us (8%)
  starting transfers between devices  18 us (6%)
  other arithmetic  15.4 us (5%)
  between operations  13.9 us (4%)
    pallas_call x1, Pallas kernels, attention_rows(): pl.pallas_call(attention_kernel, grid=(rows, cols), in_specs=[pl.BlockSpe...  67.2 us
    all_gather x1, blocking collectives, body(): line = lax.all_gather(own_bias, 'col', axis=0, tiled=True)  47 us
    reduce_scatter x1, waiting for transfers between devices, body(): lax.psum_scatter(line_grad, 'col', scatter_dimension=0, tiled=True)  39.9 us
    reduce_scatter x1, waiting for transfers between devices, body(): line_grad = lax.psum_scatter(square, 'row', scatter_dimension=0, tiled=True)  26.8 us
    all_gather x1, blocking collectives, body(): whole = lax.all_gather(line, 'row', axis=0, tiled=True)  22.7 us
    pallas_call x2, Pallas kernels, pair_call(): pl.pallas_call(kernel, grid=(rows // tile,), in_specs=[pl.BlockSpec(memor...  14.9 us
    all_to_all x2, starting transfers between devices, exchange(): lax.all_to_all(packed, 'col', split_axis=0, concat_axis=0, tiled=True)  9.99 us
    unnamed x22, local copies, waits for them, and re-layouts  9.89 us
  transfers between devices with their start and end apart: 9, of which 7 were waited for; matrix products, arithmetic and copies ran while one was open for 8% of the time, Pallas kernels for 2%

profile of v4, /device:TPU:0, one launch (start us, length us, event | category | flops | bytes accessed | tf_op | source)
XLA Modules:
  0.0 314.3 jit_solution(13702731282208412030)
XLA Ops:
  7.2 1.4 pad_maximum_fusion
  9.9 6.4 %all-to-all-start = ((bf16[4,10,64,256]{3,2,1,0:T(8,128)(2,1)}), bf16[4,10,64,256]{3,2,1,0:T(8,128)(2,1)S(1)}, u32[]{:S(2)}, u32[]{:S(2)}) async-start(bf16[4,10,64,256]{3,2,1,0:T(8,128)(2,1)} %bitcast.5), calls=%async_computation | async-start | bytes 2621440 | tf_op jit(solution)/shard_map/all_to_all | solution.py:209
  16.6 3.4 %copy-done = bf16[32,512,256]{2,1,0:T(8,128)(2,1)S(1)} copy-done((bf16[32,512,256]{2,1,0:T(8,128)(2,1)S(1)}, bf16[32,512,256]{2,1,0:T(8,128)(2,1)}, u32[]{:S(2)}) %copy-start) | copy-done | bytes 8388632
  20.0 7.4 %shard_map.119 = f32[4,512,256]{2,1,0:T(8,128)S(1)} custom-call(f32[128]{0:T(128)S(1)} %reshape.72.weight_ref, bf16[32,512,256]{2,1,0:T(8,128)(2,1)S(1)} %copy-done), custom_call_target="tpu_custom_call" | custom-call | flops 33554432 | bytes 10485760 | tf_op jit(solution)/shard_map/pallas_call | solution.py:170
  28.6 1.7 collective-permute-start.2
  30.3 1.5 collective-permute-start.1
  37.3 5.8 %collective-permute-done.1 = f16[512,256]{1,0:T(8,128)(2,1)} collective-permute-done((f16[512,256]{1,0:T(8,128)(2,1)S(1)}, f16[512,256]{1,0:T(8,128)(2,1)}, u32[]{:S(2)}, u32[]{:S(2)}) %collective-permute-start.1) | collective-permute-done | bytes 262176 | tf_op jit(solution)/shard_map/ppermute | solution.py:226
  44.4 3.4 %all-to-all-done.qk_ref = bf16[4,10,64,256]{3,2,1,0:T(8,128)(2,1)S(1)} async-done(((bf16[4,10,64,256]{3,2,1,0:T(8,128)(2,1)}), bf16[4,10,64,256]{3,2,1,0:T(8,128)(2,1)S(1)}, u32[]{:S(2)}, u32[]{:S(2)}) %all-to-all-start) | async-done | bytes 1310752 | tf_op jit(solution)/shard_map/all_to_all | solution.py:209
  47.7 3.5 %all-to-all-start.1 = ((bf16[4,10,64,256]{3,2,1,0:T(8,128)(2,1)}), bf16[4,10,64,256]{3,2,1,0:T(8,128)(2,1)S(1)}, u32[]{:S(2)}, u32[]{:S(2)}) async-start(bf16[4,10,64,256]{3,2,1,0:T(8,128)(2,1)} %bitcast.40), calls=%async_computation.1 | async-start | bytes 2621440 | tf_op jit(solution)/shard_map/all_to_all | solution.py:209
  52.0 47.0 %all-gather.6 = f16[1024,512]{0,1:T(8,128)(2,1)S(1)} all-gather(f16[256,512]{0,1:T(8,128)(2,1)S(1)} %fusion.8), channel_id=1, replica_groups=mesh['row'=2,'col'=4,'head'=4] {'col'}, dimensions={0}, use_global_device_ids=true | all-gather | bytes 1310720 | tf_op jit(solution)/shard_map/all_gather | solution.py:231
  99.0 22.7 %all-gather.7 = f16[2048,512]{0,1:T(8,128)(2,1)S(1)} all-gather(f16[1024,512]{0,1:T(8,128)(2,1)S(1)} %all-gather.6), channel_id=1, replica_groups=mesh['row'=2,'col'=4,'head'=4] {'row'}, dimensions={0}, use_global_device_ids=true | all-gather | bytes 3145728 | tf_op jit(solution)/shard_map/all_gather | solution.py:232
  121.8 2.6 convert_multiply_fusion
  124.4 5.3 %copy.22 = f32[2048,512]{1,0:T(8,128)} copy(f32[2048,512]{0,1:T(8,128)} %convert_multiply_fusion) | data formatting | bytes 8388608 | tf_op jit(solution)/shard_map/mul | solution.py:239
  129.7 4.6 %broadcast_select_fusion.bias_ref = f32[2,4,256,512]{3,2,1,0:T(8,128)} fusion(f32[2,4,256,512]{3,2,1,0:T(8,128)} %bitcast.37, pred[4,256]{1,0:T(4,128)(4,1)S(1)} %add_compare_fusion), kind=kLoop, calls=%fused_computation.2 | loop fusion | flops 1048576 | bytes 8389632 | tf_op jit(solution)/shard_map/jit(_where)/select_n | solution.py:239
  135.4 2.2 copy-done.1
  138.9 67.2 %shard_map.120 = (bf16[4,10,128,256]{3,2,1,0:T(8,128)(2,1)}, bf16[2,4,256,512]{3,2,1,0:T(8,128)(2,1)S(1)}) custom-call(s32[1]{0:T(128)} %bitcast.count_ref, bf16[4,10,64,256]{3,2,1,0:T(8,128)(2,1)S(1)} %all-to-all-done.qk_ref, bf16[4,10,64,256]{3,2,1,0:T(8,128)(2,1)S(1)} %copy-done.3, f32[2,4,256,512]{3,2,1,0:T(8,128)S(1)} %copy-done.1), custom_call_target="tpu_custom_call" | custom-call | flops 4026531840 | bytes 11534336 | tf_op jit(solution)/shard_map/pallas_call | solution.py:109
  206.1 2.5 copy.24
  208.6 4.6 %all-to-all-start.2 = ((bf16[4,10,128,256]{3,2,1,0:T(8,128)(2,1)}), bf16[4,10,128,256]{3,2,1,0:T(8,128)(2,1)}, u32[]{:S(2)}, u32[]{:S(2)}) async-start(bf16[4,10,128,256]{3,2,1,0:T(8,128)(2,1)} %get-tuple-element.17), calls=%async_computation.2 | async-start | bytes 5242880 | tf_op jit(solution)/shard_map/all_to_all | solution.py:243
  213.2 26.8 %reduce-scatter.3.cloned.1.call-done = bf16[1024,512]{0,1:T(8,128)(2,1)} async-done(((bf16[2048,512]{0,1:T(8,128)(2,1)}), bf16[1024,512]{0,1:T(8,128)(2,1)}) %reduce-scatter.3.cloned.1.call-update) | async-done | bytes 1048592 | tf_op jit(solution)/shard_map/reduce_scatter | solution.py:250
  240.1 39.9 %reduce-scatter.5.cloned.1.call-done = bf16[256,512]{0,1:T(8,128)(2,1)} async-done(((bf16[1024,512]{0,1:T(8,128)(2,1)}), bf16[256,512]{0,1:T(8,128)(2,1)}) %reduce-scatter.5.cloned.1.call-update) | async-done | bytes 262160 | tf_op jit(solution)/shard_map/reduce_scatter | solution.py:251
  279.9 6.1 %all-to-all-done.2 = bf16[4,10,128,256]{3,2,1,0:T(8,128)(2,1)} async-done(((bf16[4,10,128,256]{3,2,1,0:T(8,128)(2,1)}), bf16[4,10,128,256]{3,2,1,0:T(8,128)(2,1)}, u32[]{:S(2)}, u32[]{:S(2)}) %all-to-all-start.2) | async-done | bytes 2621472 | tf_op jit(solution)/shard_map/all_to_all | solution.py:243
  286.1 3.2 %copy.26 = bf16[40,4,32,256]{3,0,2,1:T(8,128)(2,1)S(1)} copy(bf16[40,4,32,256]{3,2,1,0:T(8,128)(2,1)} %bitcast.17) | data formatting | bytes 5242880 | tf_op jit(solution)/shard_map/reshape | solution.py:244
  292.7 6.3 %all-gather.5.cloned.1.call-done = bf16[2048,256]{1,0:T(8,128)(2,1)} async-done(((bf16[512,256]{1,0:T(8,128)(2,1)}), bf16[2048,256]{1,0:T(8,128)(2,1)}) %all-gather.5.cloned.1.call-update) | async-done | bytes 1048592 | tf_op jit(solution)/shard_map/all_gather | solution.py:252
  300.2 7.5 %shard_map.121 = bf16[32,512,256]{2,1,0:T(8,128)(2,1)} custom-call(f32[128]{0:T(128)S(1)} %reshape.72.weight_ref, bf16[4,512,256]{2,1,0:T(8,128)(2,1)S(1)} %bitcast.36), custom_call_target="tpu_custom_call" | custom-call | flops 33554432 | bytes 10485760 | tf_op jit(solution)/shard_map/pallas_call | solution.py:170
  (44 shorter events, 17.3 us)
Async XLA Ops:
  9.9 6.5 %copy-start.9 = (bf16[32,4]{0,1:T(4,128)(2,1)S(1)}, bf16[32,4]{0,1:T(4,128)(2,1)}, u32[]{:S(2)}) copy-start(bf16[32,4]{0,1:T(4,128)(2,1)} %param.14) | copy-start | bytes 772
  9.9 37.8 %all-to-all-start = ((bf16[4,10,64,256]{3,2,1,0:T(8,128)(2,1)}), bf16[4,10,64,256]{3,2,1,0:T(8,128)(2,1)S(1)}, u32[]{:S(2)}, u32[]{:S(2)}) async-start(bf16[4,10,64,256]{3,2,1,0:T(8,128)(2,1)} %bitcast.5), calls=%async_computation | async-start | bytes 2621440 | tf_op jit(solution)/shard_map/all_to_all | solution.py:209
  16.6 3.4 %copy-start = (bf16[32,512,256]{2,1,0:T(8,128)(2,1)S(1)}, bf16[32,512,256]{2,1,0:T(8,128)(2,1)}, u32[]{:S(2)}) copy-start(bf16[32,512,256]{2,1,0:T(8,128)(2,1)} %pair_ref) | copy-start | bytes 25165828
  27.6 4.3 %copy-start.5 = (bf16[1,32,40,256]{3,2,1,0:T(8,128)(2,1)S(1)}, bf16[1,32,40,256]{3,2,1,0:T(8,128)(2,1)}, u32[]{:S(2)}) copy-start(bf16[1,32,40,256]{3,2,1,0:T(8,128)(2,1)} %param.12) | copy-start | bytes 1966084
  27.6 4.3 %copy-start.7 = (bf16[1,32,40,256]{3,2,1,0:T(8,128)(2,1)S(1)}, bf16[1,32,40,256]{3,2,1,0:T(8,128)(2,1)}, u32[]{:S(2)}) copy-start(bf16[1,32,40,256]{3,2,1,0:T(8,128)(2,1)} %param.11) | copy-start | bytes 1966084
  28.6 4.5 %copy-start.10 = (s32[8]{0:T(128)S(1)}, s32[8]{0:T(128)}, u32[]{:S(2)}) copy-start(s32[8]{0:T(128)} %param.15) | copy-start | bytes 100
  28.6 7.9 %collective-permute-start = (f16[512,256]{1,0:T(8,128)(2,1)}, f16[512,256]{1,0:T(8,128)(2,1)S(1)}, u32[]{:S(2)}, u32[]{:S(2)}) collective-permute-start(f16[512,256]{1,0:T(8,128)(2,1)} %get-tuple-element.22), channel_id=1, source_target_pairs={{0,1},{1,2},{2,3},{3,0},{4,5},{5,6},{6,7},{7,4},{8,9},{9,10},{10,1... | collective-permute-start | bytes 786440 | tf_op jit(solution)/shard_map/ppermute | solution.py:226
  28.6 8.7 %collective-permute-start.2 = (f16[512,256]{1,0:T(8,128)(2,1)}, f16[512,256]{1,0:T(8,128)(2,1)}, u32[]{:S(2)}, u32[]{:S(2)}) collective-permute-start(f16[512,256]{1,0:T(8,128)(2,1)} %get-tuple-element.23), channel_id=1, source_target_pairs={{0,3},{1,0},{2,1},{3,2},{4,7},{5,4},{6,5},{7,6},{8,11},{9,8},{10,9... | collective-permute-start | bytes 786440 | tf_op jit(solution)/shard_map/ppermute | solution.py:226
  30.3 12.8 %collective-permute-start.1 = (f16[512,256]{1,0:T(8,128)(2,1)S(1)}, f16[512,256]{1,0:T(8,128)(2,1)}, u32[]{:S(2)}, u32[]{:S(2)}) collective-permute-start(f16[512,256]{1,0:T(8,128)(2,1)S(1)} %get-tuple-element.24), channel_id=1, source_target_pairs={{0,2},{1,3},{2,0},{3,1},{4,6},{5,7},{6,4},{7,5},{8,10},{9,11},{10,... | collective-permute-start | bytes 786440 | tf_op jit(solution)/shard_map/ppermute | solution.py:226
  47.7 86.6 %all-to-all-start.1 = ((bf16[4,10,64,256]{3,2,1,0:T(8,128)(2,1)}), bf16[4,10,64,256]{3,2,1,0:T(8,128)(2,1)S(1)}, u32[]{:S(2)}, u32[]{:S(2)}) async-start(bf16[4,10,64,256]{3,2,1,0:T(8,128)(2,1)} %bitcast.40), calls=%async_computation.1 | async-start | bytes 2621440 | tf_op jit(solution)/shard_map/all_to_all | solution.py:209
  51.3 188.7 %reduce-scatter.3.cloned.1.call-start = ((), (), s32[]{:S(2)}) async-start(), calls=%async_computation.5 | async-start | bytes 3145728 | tf_op jit(solution)/shard_map/reduce_scatter | solution.py:250
  134.4 1.1 copy-start.2
  135.4 2.2 copy-start.1
  137.6 1.3 copy-start.3
  208.6 77.5 %all-to-all-start.2 = ((bf16[4,10,128,256]{3,2,1,0:T(8,128)(2,1)}), bf16[4,10,128,256]{3,2,1,0:T(8,128)(2,1)}, u32[]{:S(2)}, u32[]{:S(2)}) async-start(bf16[4,10,128,256]{3,2,1,0:T(8,128)(2,1)} %get-tuple-element.17), calls=%async_computation.2 | async-start | bytes 5242880 | tf_op jit(solution)/shard_map/all_to_all | solution.py:243
  213.2 66.7 %reduce-scatter.5.cloned.1.call-start = ((), (), s32[]{:S(2)}) async-start(), calls=%async_computation.6 | async-start | bytes 1310720 | tf_op jit(solution)/shard_map/reduce_scatter | solution.py:251
  240.0 59.0 %all-gather.5.cloned.1.call-start = ((), (), s32[]{:S(2)}) async-start(), calls=%async_computation.7 | async-start | bytes 1310720 | tf_op jit(solution)/shard_map/all_gather | solution.py:252
  289.3 1.4 copy-start.6
  289.3 2.0 copy-start.8
  299.0 1.2 copy-start.4
Sparse Core Ops, SparseCore 0:
  208.7 31.2 reduce-scatter.2
  242.4 37.4 reduce-scatter.4
  281.5 17.4 all-gather.4

commit v5 on v4

--- a/solution.py
+++ b/solution.py
@@ -4,6 +4,7 @@
 import jax.numpy as jnp
 from jax import lax
 from jax.experimental import pallas as pl
+from jax.experimental.layout import Layout, with_layout_constraint
 from jax.experimental.pallas import tpu as pltpu
 from jax.sharding import PartitionSpec as P
 
@@ -50,9 +51,14 @@
     def variant(live_blocks):
         q = qk_ref[col, 0, 0:d, :]
         out_grad = va_ref[col, 0, d:2 * d, :]
+        scaled = q.astype(jnp.float32) * (SCALE * LOG2E)
+        high = scaled.astype(jnp.bfloat16)
+        low = (scaled - high.astype(jnp.float32)).astype(jnp.bfloat16)
+        pair = jnp.concatenate([high, low], axis=0)
         top = None
         for b in range(live_blocks):
-            s = contract(key(b), q, 0, 0) * (SCALE * LOG2E) + bias_ref[side, b, :, lanes]
+            twice = jnp.concatenate([key(b), key(b)], axis=0)
+            s = contract(twice, pair, 0, 0) + bias_ref[b, side, :, lanes]
             s_ref[b] = s
             block_top = jnp.max(s, axis=0, keepdims=True)
             top = block_top if top is None else jnp.maximum(top, block_top)
@@ -71,10 +77,20 @@
             dv_ref[b] += contract(out_grad, pb, 1, 1)
         out_ref[col, 0, 3 * d:4 * d, :] = attended.astype(jnp.bfloat16)
         delta = jnp.sum(out_grad.astype(jnp.float32) * attended, axis=0, keepdims=True)
+        rest = -delta
+        thirds = []
+        for _ in range(3):
+            third = rest.astype(jnp.bfloat16).astype(jnp.float32)
+            thirds.append(third)
+            rest = rest - third
+        place = lax.broadcasted_iota(jnp.int32, q.shape, 0)
+        extra = jnp.where(place == 0, thirds[0], jnp.where(place == 1, thirds[1], 0.0))
+        extra = jnp.where(place == 2, thirds[2], extra).astype(jnp.bfloat16)
+        longer = jnp.concatenate([out_grad, extra], axis=0)
+        ones = jnp.ones(q.shape, jnp.bfloat16)
         dq = jnp.zeros(q.shape, jnp.float32)
         for b in range(live_blocks):
-            dp = contract(value(b), out_grad, 0, 0)
-            ds = s_ref[b] * (dp - delta)
+            ds = s_ref[b] * contract(jnp.concatenate([value(b), ones], axis=0), longer, 0, 0)
             grad_ref[side, b, :, lanes] += ds
             dsb = ds.astype(jnp.bfloat16)
             dq = dq + contract(key(b), dsb, 1, 0)
@@ -106,20 +122,22 @@
     half_spec = pl.BlockSpec((cols, 1, depth, width), lambda i, j: (0, i, 0, 0))
     packed_spec = pl.BlockSpec((cols, 1, 2 * depth, width), lambda i, j: (0, i, 0, 0))
     bias_spec = pl.BlockSpec(bias.shape, lambda i, j: (0, 0, 0, 0))
+    square = (bias.shape[1], bias.shape[0]) + bias.shape[2:]
+    square_spec = pl.BlockSpec(square, lambda i, j: (0, 0, 0, 0))
     return pl.pallas_call(
         attention_kernel,
         grid=(rows, cols),
         in_specs=[pl.BlockSpec(memory_space=pltpu.SMEM), half_spec, half_spec, bias_spec],
-        out_specs=[packed_spec, bias_spec],
+        out_specs=[packed_spec, square_spec],
         out_shape=[
             jax.ShapeDtypeStruct((cols, rows, 2 * depth, width), jnp.bfloat16),
-            jax.ShapeDtypeStruct(bias.shape, jnp.bfloat16),
+            jax.ShapeDtypeStruct(square, jnp.bfloat16),
         ],
         scratch_shapes=[
             pltpu.VMEM((cols, width, width), jnp.float32),
             pltpu.VMEM((cols, d, width), jnp.float32),
             pltpu.VMEM((cols, d, width), jnp.float32),
-            pltpu.VMEM(bias.shape, jnp.float32),
+            pltpu.VMEM(square, jnp.float32),
         ],
         compiler_params=pltpu.CompilerParams(vmem_limit_bytes=40 * 1024 * 1024),
         cost_estimate=pl.CostEstimate(
@@ -225,17 +243,19 @@
         perm = [(i, (i + shift) % head_count) for i in range(head_count)]
         own_bias = own_bias + lax.ppermute(sent, "head", perm).astype(jnp.float32)
     own_bias = own_bias.T.astype(jnp.float16)
+    own_bias = with_layout_constraint(own_bias, Layout(major_to_minor=(0, 1)))
     va = pack((value_vectors, (cot * gate).astype(jnp.bfloat16)))
     own_bias, qk, va = lax.optimization_barrier((own_bias, qk, va))
     va = exchange(va)
-    line = lax.all_gather(own_bias, "col", axis=0, tiled=True)
-    whole = lax.all_gather(line, "row", axis=0, tiled=True)
-    whole = whole.reshape(row_count, col_count, col_block, row_block)
+    line = lax.all_gather(own_bias, "row", axis=0, tiled=True)
+    whole = lax.all_gather(line, "col", axis=0, tiled=True)
+    whole = with_layout_constraint(whole, Layout(major_to_minor=(0, 1)))
+    whole = whole.reshape(col_count, row_count, col_block, row_block)
     position = (
         jnp.arange(col_count, dtype=jnp.int32)[:, None] * col_block
         + jnp.arange(col_block, dtype=jnp.int32)[None, :]
     )
-    live = (position < count[0])[None, :, :, None]
+    live = (position < count[0])[:, None, :, None]
     bias = jnp.where(live, whole.astype(jnp.float32) * LOG2E, NEG)
 
     grads, square = attention_rows(count, qk, va, bias)

time: 309 us -> 295 us (0.955); the launches traced: 314 us -> 294 us
  blocking collectives: 69.7 us -> 60.6 us
  Pallas kernels: 82.1 us -> 75.5 us
  local copies, waits for them, and re-layouts: 26.1 us -> 20.8 us
    all_gather x2, blocking collectives: 69.7 us -> 60.6 us  [the longest x1 53.6 us: body(): whole = lax.all_gather(line, 'col', axis=0, tiled=True)]
    pallas_call x1, Pallas kernels: 67.2 us -> 60.6 us  [attention_rows(): pl.pallas_call(attention_kernel, grid=(rows, cols), in_specs=[pl.BlockSpe...]
    mul x1 -> x0, local copies, waits for them, and re-layouts: 5.33 us -> none  [body(): bias = jnp.where(live, whole.astype(jnp.float32) * LOG2E, NEG)]
    all_gather x1, waiting for transfers between devices: 6.33 us -> 9.89 us  [body(): every_head = lax.all_gather(own_grad, 'head', axis=0, tiled=False)]
    all_to_all x2, waiting for transfers between devices: 3.35 us -> 0.01 us  [exchange(): lax.all_to_all(packed, 'col', split_axis=0, concat_axis=0, tiled=True)]
  transfers between devices with their start and end apart: 9 -> 9, of which waited for: 7 -> 6; matrix products, arithmetic and copies ran while one was open for 8% -> 6% of each run, Pallas kernels for 2% -> 3%
where the time goes in v5:
time: 295 us; the launch traced here: 294 us
  waiting for transfers between devices  90.5 us (31%)
  Pallas kernels  75.5 us (26%)
  blocking collectives  60.6 us (21%)
  local copies, waits for them, and re-layouts  20.8 us (7%)
  starting transfers between devices  19.8 us (7%)
  between operations  13.8 us (5%)
  other arithmetic  12.9 us (4%)
    pallas_call x1, Pallas kernels, attention_rows(): pl.pallas_call(attention_kernel, grid=(rows, cols), in_specs=[pl.BlockSpe...  60.6 us
    all_gather x1, blocking collectives, body(): whole = lax.all_gather(line, 'col', axis=0, tiled=True)  53.6 us
    reduce_scatter x1, waiting for transfers between devices, body(): lax.psum_scatter(line_grad, 'col', scatter_dimension=0, tiled=True)  39.3 us
    reduce_scatter x1, waiting for transfers between devices, body(): line_grad = lax.psum_scatter(square, 'row', scatter_dimension=0, tiled=True)  28.6 us
    pallas_call x2, Pallas kernels, pair_call(): pl.pallas_call(kernel, grid=(rows // tile,), in_specs=[pl.BlockSpec(memor...  14.9 us
    all_to_all x2, starting transfers between devices, exchange(): lax.all_to_all(packed, 'col', split_axis=0, concat_axis=0, tiled=True)  11.6 us
    all_gather x1, waiting for transfers between devices, body(): every_head = lax.all_gather(own_grad, 'head', axis=0, tiled=False)  9.89 us
    unnamed x22, local copies, waits for them, and re-layouts  9.87 us
  transfers between devices with their start and end apart: 9, of which 6 were waited for; matrix products, arithmetic and copies ran while one was open for 6% of the time, Pallas kernels for 3%

profile of v5, /device:TPU:0, one launch (start us, length us, event | category | flops | bytes accessed | tf_op | source)
XLA Modules:
  0.0 293.9 jit_solution(14014513417964517044)
XLA Ops:
  7.2 1.4 pad_maximum_fusion
  9.9 6.4 %all-to-all-start = ((bf16[4,10,64,256]{3,2,1,0:T(8,128)(2,1)}), bf16[4,10,64,256]{3,2,1,0:T(8,128)(2,1)S(1)}, u32[]{:S(2)}, u32[]{:S(2)}) async-start(bf16[4,10,64,256]{3,2,1,0:T(8,128)(2,1)} %bitcast.5), calls=%async_computation | async-start | bytes 2621440 | tf_op jit(solution)/shard_map/all_to_all | solution.py:227
  16.6 3.4 %copy-done = bf16[32,512,256]{2,1,0:T(8,128)(2,1)S(1)} copy-done((bf16[32,512,256]{2,1,0:T(8,128)(2,1)S(1)}, bf16[32,512,256]{2,1,0:T(8,128)(2,1)}, u32[]{:S(2)}) %copy-start) | copy-done | bytes 8388632
  20.0 7.4 %shard_map.119 = f32[4,512,256]{2,1,0:T(8,128)S(1)} custom-call(f32[128]{0:T(128)S(1)} %reshape.70.weight_ref, bf16[32,512,256]{2,1,0:T(8,128)(2,1)S(1)} %copy-done), custom_call_target="tpu_custom_call" | custom-call | flops 33554432 | bytes 10485760 | tf_op jit(solution)/shard_map/pallas_call | solution.py:188
  27.3 1.8 copy.21
  29.2 1.8 convert_element_type.44
  32.0 1.7 collective-permute-start.2
  33.7 1.5 collective-permute-start.1
  37.1 1.4 pad_maximum_fusion.1
  40.7 5.8 %collective-permute-done.1 = f16[512,256]{0,1:T(8,128)(2,1)} collective-permute-done((f16[512,256]{0,1:T(8,128)(2,1)S(1)}, f16[512,256]{0,1:T(8,128)(2,1)}, u32[]{:S(2)}, u32[]{:S(2)}) %collective-permute-start.1) | collective-permute-done | bytes 262176 | tf_op jit(solution)/shard_map/ppermute | solution.py:244
  47.8 5.1 %all-to-all-start.1 = ((bf16[4,10,64,256]{3,2,1,0:T(8,128)(2,1)}), bf16[4,10,64,256]{3,2,1,0:T(8,128)(2,1)S(1)}, u32[]{:S(2)}, u32[]{:S(2)}) async-start(bf16[4,10,64,256]{3,2,1,0:T(8,128)(2,1)} %bitcast.41), calls=%async_computation.1 | async-start | bytes 2621440 | tf_op jit(solution)/shard_map/all_to_all | solution.py:227
  53.6 7.0 %all_gather.12 = f16[512,512]{1,0:T(8,128)(2,1)S(1)} all-gather(f16[256,512]{1,0:T(8,128)(2,1)S(1)} %fusion.8), channel_id=1, replica_groups=mesh['row'=2,'col'=4,'head'=4] {'row'}, dimensions={0}, use_global_device_ids=true | all-gather | bytes 786432 | tf_op jit(solution)/shard_map/all_gather | solution.py:250
  60.7 53.6 %all-gather.5 = f16[2048,512]{1,0:T(8,128)(2,1)S(1)} all-gather(f16[512,512]{1,0:T(8,128)(2,1)S(1)} %all_gather.12), channel_id=1, replica_groups=mesh['row'=2,'col'=4,'head'=4] {'col'}, dimensions={0}, use_global_device_ids=true | all-gather | bytes 2621440 | tf_op jit(solution)/shard_map/all_gather | solution.py:251
  114.9 2.5 broadcast_select_fusion.bias_ref
  118.4 2.2 copy-done.1
  121.9 60.6 %shard_map.120 = (bf16[4,10,128,256]{3,2,1,0:T(8,128)(2,1)}, bf16[2,4,256,512]{3,2,1,0:T(8,128)(2,1)S(1)}) custom-call(s32[1]{0:T(128)} %bitcast.count_ref, bf16[4,10,64,256]{3,2,1,0:T(8,128)(2,1)S(1)} %all-to-all-done.qk_ref, bf16[4,10,64,256]{3,2,1,0:T(8,128)(2,1)S(1)} %copy-done.3, f32[4,2,256,512]{3,2,1,0:T(8,128)S(1)} %copy-done.1), custom_call_target="tpu_custom_call" | custom-call | flops 4026531840 | bytes 11534336 | tf_op jit(solution)/shard_map/pallas_call | solution.py:127
  182.5 2.5 copy.24
  185.0 4.9 %all-to-all-start.2 = ((bf16[4,10,128,256]{3,2,1,0:T(8,128)(2,1)}), bf16[4,10,128,256]{3,2,1,0:T(8,128)(2,1)S(1)}, u32[]{:S(2)}, u32[]{:S(2)}) async-start(bf16[4,10,128,256]{3,2,1,0:T(8,128)(2,1)} %get-tuple-element.17), calls=%async_computation.2 | async-start | bytes 5242880 | tf_op jit(solution)/shard_map/all_to_all | solution.py:263
  189.9 28.6 %reduce-scatter.3.cloned.1.call-done = bf16[1024,512]{0,1:T(8,128)(2,1)} async-done(((bf16[2048,512]{0,1:T(8,128)(2,1)}), bf16[1024,512]{0,1:T(8,128)(2,1)}) %reduce-scatter.3.cloned.1.call-update) | async-done | bytes 1048592 | tf_op jit(solution)/shard_map/reduce_scatter | solution.py:270
  218.6 39.3 %reduce-scatter.5.cloned.1.call-done = bf16[256,512]{0,1:T(8,128)(2,1)} async-done(((bf16[1024,512]{0,1:T(8,128)(2,1)}), bf16[256,512]{0,1:T(8,128)(2,1)}) %reduce-scatter.5.cloned.1.call-update) | async-done | bytes 262160 | tf_op jit(solution)/shard_map/reduce_scatter | solution.py:271
  257.8 6.0 %all-to-all-done.2 = bf16[4,10,128,256]{3,2,1,0:T(8,128)(2,1)S(1)} async-done(((bf16[4,10,128,256]{3,2,1,0:T(8,128)(2,1)}), bf16[4,10,128,256]{3,2,1,0:T(8,128)(2,1)S(1)}, u32[]{:S(2)}, u32[]{:S(2)}) %all-to-all-start.2) | async-done | bytes 2621472 | tf_op jit(solution)/shard_map/all_to_all | solution.py:263
  263.9 1.5 copy.26
  268.7 9.9 %all-gather.4.cloned.1.call-done = bf16[2048,256]{1,0:T(8,128)(2,1)} async-done(((bf16[512,256]{1,0:T(8,128)(2,1)}), bf16[2048,256]{1,0:T(8,128)(2,1)}) %all-gather.4.cloned.1.call-update) | async-done | bytes 1048592 | tf_op jit(solution)/shard_map/all_gather | solution.py:272
  279.8 7.5 %shard_map.121 = bf16[32,512,256]{2,1,0:T(8,128)(2,1)} custom-call(f32[128]{0:T(128)S(1)} %reshape.70.weight_ref, bf16[4,512,256]{2,1,0:T(8,128)(2,1)S(1)} %bitcast.36), custom_call_target="tpu_custom_call" | custom-call | flops 33554432 | bytes 10485760 | tf_op jit(solution)/shard_map/pallas_call | solution.py:188
  (44 shorter events, 16.2 us)
Async XLA Ops:
  9.9 6.5 %copy-start.9 = (bf16[32,4]{0,1:T(4,128)(2,1)S(1)}, bf16[32,4]{0,1:T(4,128)(2,1)}, u32[]{:S(2)}) copy-start(bf16[32,4]{0,1:T(4,128)(2,1)} %param.14) | copy-start | bytes 772
  9.9 37.9 %all-to-all-start = ((bf16[4,10,64,256]{3,2,1,0:T(8,128)(2,1)}), bf16[4,10,64,256]{3,2,1,0:T(8,128)(2,1)S(1)}, u32[]{:S(2)}, u32[]{:S(2)}) async-start(bf16[4,10,64,256]{3,2,1,0:T(8,128)(2,1)} %bitcast.5), calls=%async_computation | async-start | bytes 2621440 | tf_op jit(solution)/shard_map/all_to_all | solution.py:227
  16.6 3.4 %copy-start = (bf16[32,512,256]{2,1,0:T(8,128)(2,1)S(1)}, bf16[32,512,256]{2,1,0:T(8,128)(2,1)}, u32[]{:S(2)}) copy-start(bf16[32,512,256]{2,1,0:T(8,128)(2,1)} %pair_ref) | copy-start | bytes 25165828
  31.0 4.3 %copy-start.5 = (bf16[1,32,40,256]{3,2,1,0:T(8,128)(2,1)S(1)}, bf16[1,32,40,256]{3,2,1,0:T(8,128)(2,1)}, u32[]{:S(2)}) copy-start(bf16[1,32,40,256]{3,2,1,0:T(8,128)(2,1)} %param.12) | copy-start | bytes 1966084
  31.0 4.2 %copy-start.7 = (bf16[1,32,40,256]{3,2,1,0:T(8,128)(2,1)S(1)}, bf16[1,32,40,256]{3,2,1,0:T(8,128)(2,1)}, u32[]{:S(2)}) copy-start(bf16[1,32,40,256]{3,2,1,0:T(8,128)(2,1)} %param.11) | copy-start | bytes 1966084
  32.0 4.5 %copy-start.10 = (s32[8]{0:T(128)S(1)}, s32[8]{0:T(128)}, u32[]{:S(2)}) copy-start(s32[8]{0:T(128)} %param.15) | copy-start | bytes 100
  32.0 7.9 %collective-permute-start = (f16[512,256]{0,1:T(8,128)(2,1)}, f16[512,256]{0,1:T(8,128)(2,1)}, u32[]{:S(2)}, u32[]{:S(2)}) collective-permute-start(f16[512,256]{0,1:T(8,128)(2,1)} %get-tuple-element.22), channel_id=1, source_target_pairs={{0,1},{1,2},{2,3},{3,0},{4,5},{5,6},{6,7},{7,4},{8,9},{9,10},{10,1... | collective-permute-start | bytes 786440 | tf_op jit(solution)/shard_map/ppermute | solution.py:244
  32.0 8.7 %collective-permute-start.2 = (f16[512,256]{0,1:T(8,128)(2,1)}, f16[512,256]{0,1:T(8,128)(2,1)}, u32[]{:S(2)}, u32[]{:S(2)}) collective-permute-start(f16[512,256]{0,1:T(8,128)(2,1)} %get-tuple-element.23), channel_id=1, source_target_pairs={{0,3},{1,0},{2,1},{3,2},{4,7},{5,4},{6,5},{7,6},{8,11},{9,8},{10,9... | collective-permute-start | bytes 786440 | tf_op jit(solution)/shard_map/ppermute | solution.py:244
  33.7 12.8 %collective-permute-start.1 = (f16[512,256]{0,1:T(8,128)(2,1)S(1)}, f16[512,256]{0,1:T(8,128)(2,1)}, u32[]{:S(2)}, u32[]{:S(2)}) collective-permute-start(f16[512,256]{0,1:T(8,128)(2,1)S(1)} %get-tuple-element.24), channel_id=1, source_target_pairs={{0,2},{1,3},{2,0},{3,1},{4,6},{5,7},{6,4},{7,5},{8,10},{9,11},{10,... | collective-permute-start | bytes 786440 | tf_op jit(solution)/shard_map/ppermute | solution.py:244
  47.8 69.5 %all-to-all-start.1 = ((bf16[4,10,64,256]{3,2,1,0:T(8,128)(2,1)}), bf16[4,10,64,256]{3,2,1,0:T(8,128)(2,1)S(1)}, u32[]{:S(2)}, u32[]{:S(2)}) async-start(bf16[4,10,64,256]{3,2,1,0:T(8,128)(2,1)} %bitcast.41), calls=%async_computation.1 | async-start | bytes 2621440 | tf_op jit(solution)/shard_map/all_to_all | solution.py:227
  52.9 165.6 %reduce-scatter.3.cloned.1.call-start = ((), (), s32[]{:S(2)}) async-start(), calls=%async_computation.5 | async-start | bytes 3145728 | tf_op jit(solution)/shard_map/reduce_scatter | solution.py:270
  117.3 1.1 copy-start.2
  118.4 2.2 copy-start.1
  120.6 1.3 copy-start.3
  185.0 78.9 %all-to-all-start.2 = ((bf16[4,10,128,256]{3,2,1,0:T(8,128)(2,1)}), bf16[4,10,128,256]{3,2,1,0:T(8,128)(2,1)S(1)}, u32[]{:S(2)}, u32[]{:S(2)}) async-start(bf16[4,10,128,256]{3,2,1,0:T(8,128)(2,1)} %get-tuple-element.17), calls=%async_computation.2 | async-start | bytes 5242880 | tf_op jit(solution)/shard_map/all_to_all | solution.py:263
  189.9 67.9 %reduce-scatter.5.cloned.1.call-start = ((), (), s32[]{:S(2)}) async-start(), calls=%async_computation.6 | async-start | bytes 1310720 | tf_op jit(solution)/shard_map/reduce_scatter | solution.py:271
  218.5 60.1 %all-gather.4.cloned.1.call-start = ((), (), s32[]{:S(2)}) async-start(), calls=%async_computation.7 | async-start | bytes 1310720 | tf_op jit(solution)/shard_map/all_gather | solution.py:272
  265.4 1.4 copy-start.6
  265.4 2.0 copy-start.8
  278.6 1.2 copy-start.4
Sparse Core Ops, SparseCore 0:
  185.1 33.3 reduce-scatter.2
  220.9 36.8 reduce-scatter.4
  259.4 19.1 all-gather.3
